TPU v7x, 256 devices: a whole 4x4x8 slice. The times are simulated.
256 devices in a mesh: arc: 16 (over y, x_lo, core), coef: 16 (over x_hi, z).
Axes of the slice: x: 4 (x_hi: 2, x_lo: 2; x = x_hi * 2 + x_lo), y: 4, z: 8, core: 2. Of those that a mesh axis runs over, the one named last changes fastest.
Arguments:
- design: float32 [8192, 16384], P('arc', 'coef'), may hold values from -0.046875 to 0.046875
- observations: float32 [256, 8192], P('coef', 'arc'), may hold values from -30 to 30, as said below
- start_coefs: float32 [256, 16384], P('arc', 'coef'), may hold values from -3 to 3
- precond: float32 [16384], P('coef'), may hold values from 0.3 to 1.5
- taps: float32 [128], replicated, may hold values from -0.4 to 0.4
Outputs:
- coefs: float32 [256, 16384], P('arc', 'coef')
- misfit: float32 [256, 8192], P('coef', 'arc')
Inputs may be any that keep to these rules, and one draw needn't show every extreme that they name: `observations`: observations of a satellite mission with a noise level that varies along time and occasional outliers.
All inputs are finite; a program needn't handle non-finite values.
Results may differ from a plain program's by a relative error of at most 0.00026.
Values sent between devices are 32-bit elements; how exact they have to be, the bound alone decides.
A program may use at most 64 MiB of HBM per device.

v0:
```python
import jax
import jax.numpy as jnp
from jax import lax
from jax.sharding import PartitionSpec as P

NRHS = 256
ITERS = 2


huber_square = 2.25
epsilon = 1e-06


def shifted(value, axis, steps):
    count = lax.axis_size(axis)
    initial, last = (max(0, -steps), min(count, count - steps))
    return lax.ppermute(value, axis, [(source, source + steps) for source in range(initial, last)])


def make_filters(taps):
    length = taps.shape[0]
    filt = taps.at[0].add(1.0)
    source = jnp.arange(length)[:, None]
    target = jnp.arange(length)[None, :]
    offset = target - source
    first = jnp.where(offset >= 0, filt[jnp.clip(offset, 0, length - 1)], 0.0)
    second = jnp.where(offset < 0, filt[jnp.clip(offset + length, 0, length - 1)], 0.0)
    return (first, second)


def whiten(values, first, second):
    length = first.shape[0]
    edge = shifted(values[:, -length:], "arc", 1)
    blocks = values.reshape(values.shape[0], -1, length)
    before = jnp.concatenate([edge[:, None, :], blocks[:, :-1]], axis=1)
    result = jnp.einsum("kjs,st->kjt", blocks, first, precision=lax.Precision.HIGHEST)
    result = result + jnp.einsum("kjs,st->kjt", before, second, precision=lax.Precision.HIGHEST)
    return result.reshape(values.shape)


def whiten_back(values, first, second):
    length = first.shape[0]
    edge = shifted(values[:, :length], "arc", -1)
    blocks = values.reshape(values.shape[0], -1, length)
    after = jnp.concatenate([blocks[:, 1:], edge[:, None, :]], axis=1)
    result = jnp.einsum("kjt,st->kjs", blocks, first, precision=lax.Precision.HIGHEST)
    result = result + jnp.einsum("kjt,st->kjs", after, second, precision=lax.Precision.HIGHEST)
    return result.reshape(values.shape)


def body(design, observations, start_coefs, precond, taps):
    first, second = make_filters(taps)
    rhs_arc = start_coefs.shape[0]
    rhs_coef = observations.shape[0]
    total_obs = design.shape[0] * lax.axis_size("arc")
    arc_start = lax.axis_index("arc") * rhs_arc
    coef_start = lax.axis_index("coef") * rhs_coef

    def spread(values, offset):
        return lax.dynamic_update_slice(jnp.zeros((NRHS,), jnp.float32), values, (offset,))

    def project(current):
        gathered = lax.all_gather(current, "arc", axis=0, tiled=True)
        return lax.psum_scatter(
            jnp.dot(
                gathered,
                design.T,
                precision=lax.Precision.HIGHEST,
                preferred_element_type=jnp.float32,
            ),
            "coef",
            scatter_dimension=0,
            tiled=True,
        )

    def data_sum(local):
        return lax.psum(spread(local, coef_start), ("arc", "coef"))

    def data_own(values):
        return lax.dynamic_slice_in_dim(values, coef_start, rhs_coef, 0)

    coefs = start_coefs
    predicted = project(coefs)
    direction = jnp.zeros_like(coefs)
    previous_gp = jnp.ones((NRHS,), jnp.float32)
    for iteration in range(ITERS):
        residual = observations - predicted
        whitened = whiten(residual, first, second)
        scale = data_own(data_sum(jnp.sum(whitened * whitened, axis=1)) / total_obs)
        weights = 1.0 / jnp.sqrt(
            1.0 + whitened * whitened / (huber_square * scale[:, None] + epsilon)
        )
        back = whiten_back(weights * whitened, first, second)
        back_rows = lax.all_gather(back, "coef", axis=0, tiled=True)
        gradient = lax.psum_scatter(
            jnp.dot(
                back_rows,
                design,
                precision=lax.Precision.HIGHEST,
                preferred_element_type=jnp.float32,
            ),
            "arc",
            scatter_dimension=0,
            tiled=True,
        )
        conditioned = precond[None, :] * gradient
        grad_prod, grad_old = lax.psum(
            (
                spread(jnp.sum(gradient * conditioned, axis=1), arc_start),
                spread(jnp.sum(gradient * direction, axis=1), arc_start),
            ),
            ("arc", "coef"),
        )
        if iteration == 0:
            beta = jnp.zeros((NRHS,), jnp.float32)
            grad_dir = grad_prod
        else:
            beta = grad_prod / previous_gp
            grad_dir = grad_prod + beta * grad_old
        beta_own = lax.dynamic_slice_in_dim(beta, arc_start, rhs_arc, 0)
        direction = conditioned + beta_own[:, None] * direction
        image = project(direction)
        imaged = whiten(image, first, second)
        curvature = data_sum(jnp.sum(weights * imaged * imaged, axis=1))
        alpha = grad_dir / curvature
        alpha_arc = lax.dynamic_slice_in_dim(alpha, arc_start, rhs_arc, 0)
        coefs = coefs + alpha_arc[:, None] * direction
        predicted = predicted + data_own(alpha)[:, None] * image
        previous_gp = grad_prod
    misfit = observations - predicted
    return (coefs, misfit)


def solution(mesh):
    placed = (P("arc", "coef"), P("coef", "arc"), P("arc", "coef"), P("coef"), P())
    return jax.shard_map(
        body,
        mesh=mesh,
        in_specs=placed,
        out_specs=(P("arc", "coef"), P("coef", "arc")),
        check_vma=False,
    )
```

profile of v0, /device:TPU:24, one launch (start us, length us, event | category | flops | bytes accessed | tf_op | source)
XLA Modules:
  0.0 1344.3 jit_solution(11943564390350085950)
XLA Ops:
  8.0 38.6 %all-gather.4.cloned.1.call-done = f32[256,1024]{1,0:T(8,128)} async-done(((f32[16,1024]{1,0:T(8,128)}), f32[256,1024]{1,0:T(8,128)}) %all-gather.4.cloned.1.call-update) | async-done | bytes 1048592 | tf_op jit(solution)/shard_map/all_gather | solution.py:63
  46.6 4.0 fusion.90
  50.7 97.2 %gather_fusion = f32[16384]{0:T(1024)S(1)} fusion(f32[128]{0:T(128)S(1)} %add_dynamic-update-slice_fusion, s32[16384]{0:T(1024)S(1)} %fusion.4), kind=kCustom, calls=%fused_computation | custom fusion | bytes 196608 | tf_op jit(solution)/shard_map/gather | solution.py:26
  148.0 97.2 %gather_fusion.1 = f32[16384]{0:T(1024)S(1)} fusion(f32[128]{0:T(128)S(1)} %add_dynamic-update-slice_fusion, s32[16384]{0:T(1024)S(1)} %fusion.6), kind=kCustom, calls=%fused_computation.1 | custom fusion | bytes 196608 | tf_op jit(solution)/shard_map/gather | solution.py:27
  245.2 4.2 reduce-scatter.6.cloned.1.call-done
  252.3 3.9 collective-permute-done
  256.7 72.2 %psum.49 = f32[256]{0:T(256)S(1)} all-reduce(f32[256]{0:T(256)S(1)} %dynamic_update_slice.21), channel_id=1, replica_groups=mesh['arc'=16,'coef'=16] {'arc','coef'}, use_global_device_ids=true, to_apply=%region_2.3 | all-reduce | flops 256 | bytes 2048 | tf_op jit(solution)/shard_map/psum | solution.py:77
  332.7 42.1 %all_gather.16 = f32[256,512]{1,0:T(8,128)S(1)} all-gather(f32[16,512]{1,0:T(8,128)S(1)} %bitcast.164), channel_id=1, replica_groups=mesh['arc'=16,'coef'=16] {'coef'}, dimensions={0}, use_global_device_ids=true | all-gather | bytes 557056 | tf_op jit(solution)/shard_map/all_gather | solution.py:94
  374.9 2.9 fusion.91
  377.8 53.2 %reduce-scatter.8.cloned.1.call-done = f32[16,1024]{1,0:T(8,128)} async-done(((f32[256,1024]{1,0:T(8,128)}), f32[16,1024]{1,0:T(8,128)}) %reduce-scatter.8.cloned.1.call-update) | async-done | bytes 65552 | tf_op jit(solution)/shard_map/reduce_scatter | solution.py:95
  432.7 40.1 %all-gather.6.cloned.1.call-done = f32[256,1024]{1,0:T(8,128)} async-done(((f32[16,1024]{1,0:T(8,128)}), f32[256,1024]{1,0:T(8,128)}) %all-gather.6.cloned.1.call-update) | async-done | bytes 1048592 | tf_op jit(solution)/shard_map/all_gather | solution.py:63
  472.8 4.0 fusion.92
  477.1 198.3 %reduce-scatter.10.cloned.1.call-done = f32[16,512]{1,0:T(8,128)} async-done(((f32[256,512]{1,0:T(8,128)}), f32[16,512]{1,0:T(8,128)}) %reduce-scatter.10.cloned.1.call-update) | async-done | bytes 32784 | tf_op jit(solution)/shard_map/reduce_scatter | solution.py:64
  682.6 72.8 %all-reduce.1 = (f32[256]{0:T(256)S(1)}, f32[256]{0:T(256)S(1)}) all-reduce(f32[256]{0:T(256)S(1)} %dynamic_update_slice.22, f32[256]{0:T(256)S(1)} %dynamic_update_slice.23), channel_id=1, replica_groups=mesh['arc'=16,'coef'=16] {'arc','coef'}, use_global_device_ids=true, to_apply=%region_5.6 | all-reduce | flops 512 | bytes 4096 | tf_op jit(solution)/shard_map/psum | solution.py:107
  758.5 3.9 collective-permute-done.3
  763.0 72.5 %psum.52 = f32[256]{0:T(256)S(1)} all-reduce(f32[256]{0:T(256)S(1)} %dynamic_update_slice.24), channel_id=1, replica_groups=mesh['arc'=16,'coef'=16] {'arc','coef'}, use_global_device_ids=true, to_apply=%region_10.11 | all-reduce | flops 256 | bytes 2048 | tf_op jit(solution)/shard_map/psum | solution.py:77
  839.3 41.0 %all_gather.18 = f32[256,512]{1,0:T(8,128)S(1)} all-gather(f32[16,512]{1,0:T(8,128)S(1)} %bitcast.165), channel_id=1, replica_groups=mesh['arc'=16,'coef'=16] {'coef'}, dimensions={0}, use_global_device_ids=true | all-gather | bytes 557056 | tf_op jit(solution)/shard_map/all_gather | solution.py:94
  880.3 2.9 fusion.93
  883.2 53.6 %reduce-scatter.12.cloned.1.call-done = f32[16,1024]{1,0:T(8,128)} async-done(((f32[256,1024]{1,0:T(8,128)}), f32[16,1024]{1,0:T(8,128)}) %reduce-scatter.12.cloned.1.call-update) | async-done | bytes 65552 | tf_op jit(solution)/shard_map/reduce_scatter | solution.py:95
  938.0 79.9 %psum.53 = f32[256]{0:T(256)S(1)} all-reduce(f32[256]{0:T(256)S(1)} %dynamic_update_slice.25), channel_id=1, replica_groups=mesh['arc'=16,'coef'=16] {'arc','coef'}, use_global_device_ids=true, to_apply=%region_13.14 | all-reduce | flops 256 | bytes 2048 | tf_op jit(solution)/shard_map/psum | solution.py:107
  1019.7 33.0 %all-gather.8.cloned.1.call-done = f32[256,1024]{1,0:T(8,128)} async-done(((f32[16,1024]{1,0:T(8,128)}), f32[256,1024]{1,0:T(8,128)}) %all-gather.8.cloned.1.call-update) | async-done | bytes 1048592 | tf_op jit(solution)/shard_map/all_gather | solution.py:63
  1052.6 4.0 fusion.94
  1056.9 198.4 %reduce-scatter.14.cloned.1.call-done = f32[16,512]{1,0:T(8,128)} async-done(((f32[256,512]{1,0:T(8,128)}), f32[16,512]{1,0:T(8,128)}) %reduce-scatter.14.cloned.1.call-update) | async-done | bytes 32784 | tf_op jit(solution)/shard_map/reduce_scatter | solution.py:64
  1262.4 72.8 %all-reduce = (f32[256]{0:T(256)S(1)}, f32[256]{0:T(256)S(1)}) all-reduce(f32[256]{0:T(256)S(1)} %dynamic_update_slice.27, f32[256]{0:T(256)S(1)} %dynamic_update_slice.26), channel_id=1, replica_groups=mesh['arc'=16,'coef'=16] {'arc','coef'}, use_global_device_ids=true, to_apply=%region_18.19 | all-reduce | flops 512 | bytes 4096 | tf_op jit(solution)/shard_map/psum | solution.py:77
  (112 shorter events, 37.1 us)
Async XLA Ops:
  7.2 39.4 %copy-start = (f32[512,1024]{1,0:T(8,128)S(1)}, f32[512,1024]{1,0:T(8,128)}, u32[]{:S(2)}) copy-start(f32[512,1024]{1,0:T(8,128)} %param.7) | copy-start | bytes 6291460
  7.2 39.4 %all-gather.4.cloned.1.call-start = ((), (), s32[]{:S(2)}) async-start(), calls=%async_computation.5 | async-start | bytes 1114112 | tf_op jit(solution)/shard_map/all_gather | solution.py:63
  7.9 42.7 %copy-start.1 = (f32[128]{0:T(128)S(1)}, f32[128]{0:T(128)}, u32[]{:S(2)}) copy-start(f32[128]{0:T(128)} %param.11) | copy-start | bytes 1540
  7.9 241.4 %reduce-scatter.6.cloned.1.call-start = ((), (), s32[]{:S(2)}) async-start(), calls=%async_computation.6 | async-start | bytes 557056 | tf_op jit(solution)/shard_map/reduce_scatter | solution.py:64
  50.6 380.4 %reduce-scatter.8.cloned.1.call-start = ((), (), s32[]{:S(2)}) async-start(), calls=%async_computation.7 | async-start | bytes 1114112 | tf_op jit(solution)/shard_map/reduce_scatter | solution.py:95
  148.0 101.4 %copy-start.5 = (f32[16,512]{1,0:T(8,128)S(1)}, f32[16,512]{1,0:T(8,128)}, u32[]{:S(2)}) copy-start(f32[16,512]{1,0:T(8,128)} %param.8) | copy-start | bytes 98308
  250.3 5.9 collective-permute-start
  329.2 3.3 collective-permute-start.1
  374.8 56.2 %copy-start.8 = (f32[1024]{0:T(1024)S(1)}, f32[1024]{0:T(1024)}, u32[]{:S(2)}) copy-start(f32[1024]{0:T(1024)} %param.10) | copy-start | bytes 12292
  377.8 95.0 %all-gather.6.cloned.1.call-start = ((), (), s32[]{:S(2)}) async-start(), calls=%async_computation.8 | async-start | bytes 1114112 | tf_op jit(solution)/shard_map/all_gather | solution.py:63
  432.6 322.8 %copy-start.6 = (f32[16,512]{1,0:T(8,128)S(1)}, f32[16,512]{1,0:T(8,128)}, u32[]{:S(2)}) copy-start(f32[16,512]{1,0:T(8,128)} %reduce-scatter.6.cloned.1.call-done) | copy-start | bytes 98308
  432.6 242.8 %reduce-scatter.10.cloned.1.call-start = ((), (), s32[]{:S(2)}) async-start(), calls=%async_computation.9 | async-start | bytes 557056 | tf_op jit(solution)/shard_map/reduce_scatter | solution.py:64
  476.8 460.0 %reduce-scatter.12.cloned.1.call-start = ((), (), s32[]{:S(2)}) async-start(), calls=%async_computation.10 | async-start | bytes 1114112 | tf_op jit(solution)/shard_map/reduce_scatter | solution.py:95
  676.1 5.9 collective-permute-start.2
  756.5 5.9 collective-permute-start.3
  835.8 3.3 collective-permute-start.4
  880.3 56.6 %copy-start.2 = (f32[16,1024]{1,0:T(8,128)S(1)}, f32[16,1024]{1,0:T(8,128)}, u32[]{:S(2)}) copy-start(f32[16,1024]{1,0:T(8,128)} %reduce-scatter.8.cloned.1.call-done) | copy-start | bytes 196612
  883.2 169.5 %all-gather.8.cloned.1.call-start = ((), (), s32[]{:S(2)}) async-start(), calls=%async_computation.11 | async-start | bytes 1114112 | tf_op jit(solution)/shard_map/all_gather | solution.py:63
  1019.6 315.7 %copy-start.3 = (f32[16,512]{1,0:T(8,128)S(1)}, f32[16,512]{1,0:T(8,128)}, u32[]{:S(2)}) copy-start(f32[16,512]{1,0:T(8,128)} %reduce-scatter.10.cloned.1.call-done) | copy-start | bytes 98308
  1019.6 317.2 %copy-start.4 = (f32[16,1024]{1,0:T(8,128)S(1)}, f32[16,1024]{1,0:T(8,128)}, u32[]{:S(2)}) copy-start(f32[16,1024]{1,0:T(8,128)} %multiply_add_fusion) | copy-start | bytes 196612
  1019.6 317.2 %copy-start.7 = (f32[16,1024]{1,0:T(8,128)S(1)}, f32[16,1024]{1,0:T(8,128)}, u32[]{:S(2)}) copy-start(f32[16,1024]{1,0:T(8,128)} %param.9) | copy-start | bytes 196612
  1019.6 235.6 %reduce-scatter.14.cloned.1.call-start = ((), (), s32[]{:S(2)}) async-start(), calls=%async_computation.12 | async-start | bytes 557056 | tf_op jit(solution)/shard_map/reduce_scatter | solution.py:64
  1256.0 5.9 collective-permute-start.5
Sparse Core Ops, SparseCore 0:
  9.9 36.6 all-gather.3
  50.7 198.6 reduce-scatter.5
  377.9 53.0 reduce-scatter.7
  433.3 39.4 all-gather.5
  476.9 198.4 reduce-scatter.9
  883.3 53.4 reduce-scatter.11
  1019.7 32.8 all-gather.7
  1056.8 198.4 reduce-scatter.13
where the time goes:
time: 1350 us; the launch traced here: 1340 us
  waiting for transfers between devices  635 us (47%)
  blocking collectives  453 us (34%)
  local copies, waits for them, and re-layouts  199 us (15%)
  matrix products  22.1 us (2%)
  between operations  14.5 us (1%)
    reduce_scatter x3, waiting for transfers between devices, project(): lax.psum_scatter(jnp.dot(gathered, design.T, precision=lax.Precision.HIGH...  401 us
    psum x3, blocking collectives, data_sum(): return lax.psum(spread(local, coef_start), ('arc', 'coef'))  218 us
    psum x2, blocking collectives, body(): lax.psum((spread(jnp.sum(gradient * conditioned, axis=1), arc_start), spr...  153 us
    all_gather x3, waiting for transfers between devices, project(): gathered = lax.all_gather(current, 'arc', axis=0, tiled=True)  112 us
    reduce_scatter x2, waiting for transfers between devices, body(): lax.psum_scatter(jnp.dot(back_rows, design, precision=lax.Precision.HIGHE...  107 us
    gather x1, local copies, waits for them, and re-layouts, make_filters(): first = jnp.where(offset >= 0, filt[jnp.clip(offset, 0, length - 1)], 0.0)  97.2 us
    gather x1, local copies, waits for them, and re-layouts, make_filters(): filt[jnp.clip(offset + length, 0, length - 1)]  97.2 us
    all_gather x2, blocking collectives, body(): back_rows = lax.all_gather(back, 'coef', axis=0, tiled=True)  83.1 us
  transfers between devices with their start and end apart: 14, of which 14 were waited for; matrix products, arithmetic and copies ran while one was open for 15% of the time, Pallas kernels for 0%

commit v1 on v0

v1 whole, which is shorter than its diff:
```python
import functools
import jax
import jax.numpy as jnp
from jax import lax
from jax.experimental import pallas as pl
from jax.experimental.pallas import tpu as pltpu
from jax.sharding import PartitionSpec as P

ITERS = 2
TOTAL_OBS = 8192
HUBER_SQUARE = 2.25
EPSILON = 1e-06

F32 = jnp.float32
BF16 = jnp.bfloat16
MESH = pl.DeviceIdType.MESH


def split(value):
    high = value.astype(BF16)
    low = (value - high.astype(F32)).astype(BF16)
    return high, low


def dot3(value, weight_high, weight_low):
    rows = value.shape[0]
    high, low = split(value)
    both = jnp.dot(jnp.concatenate([high, low], axis=0), weight_high, preferred_element_type=F32)
    rest = jnp.dot(high, weight_low, preferred_element_type=F32)
    return both[:rows] + both[rows:] + rest


def lanes(value):
    total = value[:, 0:128]
    for start in range(128, value.shape[1], 128):
        total = total + value[:, start:start + 128]
    return total


def fold(value):
    value = value + pltpu.roll(value, 64, 1)
    lane = lax.broadcasted_iota(jnp.int32, (8, 128), 1)
    return jnp.where(lane < 64, value[0:8], value[8:16])


def unfold(value):
    lane = lax.broadcasted_iota(jnp.int32, (8, 128), 1)
    upper = jnp.sum(jnp.where(lane < 64, value, 0.0), axis=1, keepdims=True)
    lower = jnp.sum(jnp.where(lane < 64, 0.0, value), axis=1, keepdims=True)
    return jnp.concatenate([upper, lower], axis=0)


def filter_blocks(extended):
    return jnp.concatenate([extended[:, j * 128:(j + 2) * 128] for j in range(4)], axis=0)


def unblock(value):
    return jnp.concatenate([value[j * 16:(j + 1) * 16] for j in range(4)], axis=1)


def kernel(design_hbm, obs_ref, start_ref, precond_ref, taps_ref, coefs_ref, misfit_ref,
           design_f, d_high, d_low, t_high, t_low, w_high, w_low, b_high, b_low,
           gather, partial, landed, back_rows, grad_part, pair_land, grad_land,
           edge_src, edge_dst, sum_src, sum_dst, gp_src, gp_dst, diag_gp, diag_alpha,
           load_sem, ag_send, ag_recv, fwd_send, fwd_recv, rs_send, rs_recv,
           bg_send, bg_recv, pair_send, pair_recv, ra_send, ra_recv,
           edge_send, edge_recv, sum_send, sum_recv, gp_send, gp_recv, diag_send, diag_recv):
    a = lax.axis_index("arc")
    c = lax.axis_index("coef")
    y, ma = a // 4, a % 4
    xlo, core = ma // 2, ma % 2
    yc, mc = c // 4, c % 4
    sibling = a + 1 - 2 * core

    load = pltpu.make_async_copy(design_hbm, design_f, load_sem)
    load.start()

    barrier = pltpu.get_barrier_semaphore()

    def greet(k, carry):
        pl.semaphore_signal(barrier, inc=1, device_id=((a + k) % 16, c), device_id_type=MESH)
        pl.semaphore_signal(barrier, inc=1, device_id=(a, (c + k) % 16), device_id_type=MESH)
        return carry

    lax.fori_loop(1, 16, greet, 0)

    def remote(src, dst, send, recv, device):
        return pltpu.make_async_remote_copy(src_ref=src, dst_ref=dst, send_sem=send, recv_sem=recv,
                                            device_id=device, device_id_type=MESH)

    def wait_bytes(ref, sem):
        pltpu.make_async_copy(ref, ref, sem).wait()

    row = lax.broadcasted_iota(jnp.int32, (128, 128), 0)
    col = lax.broadcasted_iota(jnp.int32, (128, 128), 1)
    lead = lax.broadcasted_iota(jnp.int32, (1, 128), 1)
    filt = taps_ref[...] + jnp.where(lead == 0, 1.0, 0.0)
    rolled = jnp.broadcast_to(filt, (128, 128))
    for bit in range(7):
        rolled = jnp.where((row // (1 << bit)) % 2 == 1, pltpu.roll(rolled, 1 << bit, 1), rolled)
    first = jnp.where(col >= row, rolled, 0.0)
    second = jnp.where(col < row, rolled, 0.0)
    high, low = split(jnp.concatenate([second, first], axis=0))
    w_high[...] = high
    w_low[...] = low
    high, low = split(jnp.concatenate([first.T, second.T], axis=0))
    b_high[...] = high
    b_low[...] = low

    gather[0, ma, y] = start_ref[...]

    pl.semaphore_wait(barrier, 30)

    def gather_arc(p):
        def step(k, carry):
            i, ky = k // 4, k % 4
            target = ((y + ky) % 4) * 4 + ((xlo + i) % 2) * 2 + core

            @pl.when(k > 0)
            def _():
                remote(gather.at[p, ma, y], gather.at[p, ma, y], ag_send.at[p], ag_recv.at[p, k], (target, c)).start()
            return carry

        lax.fori_loop(0, 8, step, 0)

    def forward(p):
        def step(s, carry):
            i, j = s // 2, s % 2
            m = ((xlo + i) % 2) * 2 + (core + j) % 2

            @pl.when(j == 0)
            def _():
                for ky in range(4):
                    source_y = (y + 4 - ky) % 4
                    if ky == 0:
                        @pl.when(i > 0)
                        def _():
                            wait_bytes(gather.at[p, m, source_y], ag_recv.at[p, i * 4])
                    else:
                        wait_bytes(gather.at[p, m, source_y], ag_recv.at[p, i * 4 + ky])
                    remote(gather.at[p, m, source_y], gather.at[p, m, source_y], fwd_send.at[p], fwd_recv.at[p, i], (sibling, c)).start()

            @pl.when(j == 1)
            def _():
                wait_bytes(gather.at[p, m], fwd_recv.at[p, i])

            block = gather[p, m].reshape(64, 1024)
            product = dot3(block, t_high[...], t_low[...])
            partial[p, m] = product.reshape(4, 16, 512)
            for k in range(4):
                yk = (yc + k) % 4
                owner = yk * 4 + m

                @pl.when(owner != c)
                def _():
                    remote(partial.at[p, m, yk], landed.at[p, (owner + 16 - c) % 16], rs_send.at[p], rs_recv.at[p], (a, owner)).start()
            return carry

        lax.fori_loop(0, 4, step, 0)

    def forward_sum(p):
        wait_bytes(landed.at[p, 1:16], rs_recv.at[p])
        total = partial[p, mc, yc]
        for k in range(1, 16):
            total = total + landed[p, k]
        return total

    def gather_coef(it):
        def step(k, carry):
            dz, flip = k // 2, k % 2
            dz = (dz // 2) + (dz % 2) * 4
            z, xh = c % 8, c // 8
            target = ((xh + flip) % 2) * 8 + (z + dz) % 8

            @pl.when(k > 0)
            def _():
                remote(back_rows.at[it, mc, yc], back_rows.at[it, mc, yc], bg_send.at[it], bg_recv.at[it, dz % 4], (a, target)).start()
            return carry

        lax.fori_loop(0, 16, step, 0)

    def backward(it):
        def finish(k):
            m = (mc + 4 - k) % 4
            xl, co = m // 2, m % 2

            @pl.when(co == core)
            def _():
                wait_bytes(pair_land.at[it, xl], pair_recv.at[it, xl])
                grad_part[it, m] = grad_part[it, m] + pair_land[it, xl]
                i = (xl + 2 - xlo) % 2
                for ky in range(4):
                    ty = (y + ky) % 4
                    target = ty * 4 + m

                    @pl.when(target != a)
                    def _():
                        remote(grad_part.at[it, m, ty], grad_land.at[it, i * 4 + ky], ra_send.at[it], ra_recv.at[it], (target, c)).start()

        def step(k, carry):
            m = (mc + 4 - k) % 4
            xl, co = m // 2, m % 2

            @pl.when(k == 0)
            def _():
                wait_bytes(back_rows.at[it, m, 0:3], bg_recv.at[it, 0])

            @pl.when(k > 0)
            def _():
                wait_bytes(back_rows.at[it, m], bg_recv.at[it, k])

            block = back_rows[it, m].reshape(64, 512)
            product = dot3(block, d_high[...], d_low[...])
            grad_part[it, m] = product.reshape(4, 16, 1024)

            @pl.when(co != core)
            def _():
                remote(grad_part.at[it, m], pair_land.at[it, xl], pair_send.at[it, xl], pair_recv.at[it, xl], (sibling, c)).start()

            @pl.when(k > 0)
            def _():
                finish(k - 1)
            return carry

        lax.fori_loop(0, 4, step, 0)
        finish(3)

    def backward_sum(it):
        wait_bytes(grad_land.at[it, 1:8], ra_recv.at[it])
        total = grad_part[it, ma, y]
        for k in range(1, 8):
            total = total + grad_land[it, k]
        return total

    def edge_next(n, value):
        edge_src[n] = value

        @pl.when(a < 15)
        def _():
            remote(edge_src.at[n], edge_dst.at[n], edge_send.at[n], edge_recv.at[n], (a + 1, c)).start()

        @pl.when(a == 0)
        def _():
            edge_dst[n] = jnp.zeros((16, 128), F32)

    def edge_next_wait(n):
        @pl.when(a > 0)
        def _():
            wait_bytes(edge_dst.at[n], edge_recv.at[n])
        return edge_dst[n]

    def edge_previous(n, value):
        edge_src[n] = value

        @pl.when(a > 0)
        def _():
            remote(edge_src.at[n], edge_dst.at[n], edge_send.at[n], edge_recv.at[n], (a - 1, c)).start()

        @pl.when(a == 15)
        def _():
            edge_dst[n] = jnp.zeros((16, 128), F32)

    def edge_previous_wait(n):
        @pl.when(a < 15)
        def _():
            wait_bytes(edge_dst.at[n], edge_recv.at[n])
        return edge_dst[n]

    def whiten(n, value):
        edge_next(n, value[:, 384:512])
        edge = edge_next_wait(n)
        blocks = filter_blocks(jnp.concatenate([edge, value], axis=1))
        return unblock(dot3(blocks, w_high[...], w_low[...]))

    def whiten_back(n, value):
        edge_previous(n, value[:, 0:128])
        edge = edge_previous_wait(n)
        blocks = filter_blocks(jnp.concatenate([value, edge], axis=1))
        return unblock(dot3(blocks, b_high[...], b_low[...]))

    def time_sum(n, value):
        sum_src[n] = fold(lanes(value))

        def step(k, carry):
            remote(sum_src.at[n], sum_dst.at[n, k], sum_send.at[n], sum_recv.at[n], ((a + k) % 16, c)).start()
            return carry

        lax.fori_loop(1, 16, step, 0)

    def time_sum_wait(n):
        wait_bytes(sum_dst.at[n, 1:16], sum_recv.at[n])
        total = sum_src[n]
        for k in range(1, 16):
            total = total + sum_dst[n, k]
        return unfold(total)

    def coef_sum(it, product, old):
        gp_src[it, 0:8] = fold(lanes(product))
        gp_src[it, 8:16] = fold(lanes(old))

        def step(k, carry):
            remote(gp_src.at[it], gp_dst.at[it, k], gp_send.at[it], gp_recv.at[it], (a, (c + k) % 16)).start()
            return carry

        lax.fori_loop(1, 16, step, 0)

    def coef_sum_wait(it):
        wait_bytes(gp_dst.at[it, 1:16], gp_recv.at[it])
        total = gp_src[it]
        for k in range(1, 16):
            total = total + gp_dst[it, k]

        @pl.when(a == c)
        def _():
            diag_gp[it] = total

            def step(k, carry):
                remote(diag_gp.at[it], diag_gp.at[it], diag_send.at[it, 0], diag_recv.at[it, 0], ((a + k) % 16, c)).start()
                return carry

            lax.fori_loop(1, 16, step, 0)
        return unfold(total[0:8]), unfold(total[8:16])

    def diag_gp_wait(it):
        @pl.when(a != c)
        def _():
            wait_bytes(diag_gp.at[it], diag_recv.at[it, 0])
        total = diag_gp[it]
        return unfold(total[0:8]), unfold(total[8:16])

    def alpha_spread(it, alpha):
        @pl.when(a == c)
        def _():
            diag_alpha[it] = jnp.broadcast_to(alpha, (16, 128))

            def step(k, carry):
                remote(diag_alpha.at[it], diag_alpha.at[it], diag_send.at[it, 1], diag_recv.at[it, 1], (a, (c + k) % 16)).start()
                return carry

            lax.fori_loop(1, 16, step, 0)

    def alpha_wait(it):
        @pl.when(a != c)
        def _():
            wait_bytes(diag_alpha.at[it], diag_recv.at[it, 1])
        return diag_alpha[it][:, 0:1]

    gather_arc(0)

    load.wait()

    def prepare(r, carry):
        at = pl.ds(pl.multiple_of(r * 128, 128), 128)
        piece = design_f[at, :]
        high, low = split(piece)
        d_high[at, :] = high
        d_low[at, :] = low
        high, low = split(piece.T)
        t_high[:, at] = high
        t_low[:, at] = low
        return carry

    lax.fori_loop(0, 4, prepare, 0)

    forward(0)
    observations = obs_ref[...]
    residual = observations - forward_sum(0)
    whitened = whiten(0, residual)
    time_sum(0, whitened * whitened)

    image_old = imaged_old = gp_a_old = gp_c_old = None
    betas, alphas = [], []
    for it in range(ITERS):
        scale = time_sum_wait(2 * it) * (1.0 / TOTAL_OBS)
        weights = lax.rsqrt(1.0 + whitened * whitened / (HUBER_SQUARE * scale + EPSILON))
        back = whiten_back(1 + 2 * it, weights * whitened)
        back_rows[it, mc, yc] = back
        gather_coef(it)
        backward(it)
        gradient = backward_sum(it)
        conditioned = precond_ref[...] * gradient
        gather[it + 1, ma, y] = conditioned
        gather_arc(it + 1)
        if it == 0:
            old = jnp.zeros_like(gradient)
        else:
            old = gradient * direction
        coef_sum(it, gradient * conditioned, old)
        forward(it + 1)
        gp_a, go_a = coef_sum_wait(it)
        if it == 0:
            direction = conditioned
        else:
            direction = conditioned + (gp_a / gp_a_old) * direction
        image = forward_sum(it + 1)
        imaged = whiten(2 + 2 * it, image)
        gp_c, go_c = diag_gp_wait(it)
        if it == 0:
            gd_c = gp_c
        else:
            beta_c = gp_c / gp_c_old
            gd_c = gp_c + beta_c * go_c
            image = image + beta_c * image_old
            imaged = imaged + beta_c * imaged_old
        time_sum(2 * it + 1, weights * imaged * imaged)
        alpha = gd_c / time_sum_wait(2 * it + 1)
        alpha_spread(it, alpha)
        residual = residual - alpha * image
        if it + 1 < ITERS:
            whitened = whitened - alpha * imaged
            time_sum(2 * it + 2, whitened * whitened)
        image_old, imaged_old, gp_a_old, gp_c_old = image, imaged, gp_a, gp_c
        if it == 0:
            first_direction = direction
    misfit_ref[...] = residual
    coefs = start_ref[...]
    coefs = coefs + alpha_wait(0) * first_direction
    coefs = coefs + alpha_wait(1) * direction
    coefs_ref[...] = coefs

    for p in range(ITERS + 1):
        wait_bytes(landed.at[p, 0:14], ag_send.at[p])
        wait_bytes(gather.at[p, 0:2], fwd_send.at[p])
        wait_bytes(landed.at[p, 1:16], rs_send.at[p])
    for it in range(ITERS):
        wait_bytes(landed.at[it, 1:16], bg_send.at[it])
        for xl in range(2):
            wait_bytes(pair_land.at[it, xl], pair_send.at[it, xl])
        wait_bytes(grad_land.at[it, 1:8], ra_send.at[it])
        wait_bytes(gp_dst.at[it, 1:16], gp_send.at[it])

        @pl.when(a == c)
        def _():
            wait_bytes(gp_dst.at[it, 1:16], diag_send.at[it, 0])
            wait_bytes(gp_dst.at[it, 1:16], diag_send.at[it, 1])
    for n in range(2 * ITERS):
        wait_bytes(sum_dst.at[n, 1:16], sum_send.at[n])
    for n in range(2 * ITERS + 1):
        @pl.when((a < 15) if n % 2 == 0 else (a > 0))
        def _():
            wait_bytes(edge_src.at[n], edge_send.at[n])


def body(design, observations, start_coefs, precond, taps):
    vmem = pl.BlockSpec(memory_space=pltpu.VMEM)
    dma = pltpu.SemaphoreType.DMA
    scratch = [
        pltpu.VMEM((512, 1024), F32),
        pltpu.VMEM((512, 1024), BF16), pltpu.VMEM((512, 1024), BF16),
        pltpu.VMEM((1024, 512), BF16), pltpu.VMEM((1024, 512), BF16),
        pltpu.VMEM((256, 128), BF16), pltpu.VMEM((256, 128), BF16),
        pltpu.VMEM((256, 128), BF16), pltpu.VMEM((256, 128), BF16),
        pltpu.VMEM((3, 4, 4, 16, 1024), F32),
        pltpu.VMEM((3, 4, 4, 16, 512), F32),
        pltpu.VMEM((3, 16, 16, 512), F32),
        pltpu.VMEM((2, 4, 4, 16, 512), F32),
        pltpu.VMEM((2, 4, 4, 16, 1024), F32),
        pltpu.VMEM((2, 2, 4, 16, 1024), F32),
        pltpu.VMEM((2, 8, 16, 1024), F32),
        pltpu.VMEM((5, 16, 128), F32), pltpu.VMEM((5, 16, 128), F32),
        pltpu.VMEM((4, 8, 128), F32), pltpu.VMEM((4, 16, 8, 128), F32),
        pltpu.VMEM((2, 16, 128), F32), pltpu.VMEM((2, 16, 16, 128), F32),
        pltpu.VMEM((2, 16, 128), F32), pltpu.VMEM((2, 16, 128), F32),
        dma,
        dma((3,)), dma((3, 8)), dma((3,)), dma((3, 2)), dma((3,)), dma((3,)),
        dma((2,)), dma((2, 4)), dma((2, 2)), dma((2, 2)), dma((2,)), dma((2,)),
        dma((5,)), dma((5,)), dma((4,)), dma((4,)), dma((2,)), dma((2,)), dma((2, 2)), dma((2, 2)),
    ]
    return pl.pallas_call(
        kernel,
        out_shape=(jax.ShapeDtypeStruct(start_coefs.shape, F32), jax.ShapeDtypeStruct(observations.shape, F32)),
        in_specs=[pl.BlockSpec(memory_space=pl.ANY), vmem, vmem, vmem, vmem],
        out_specs=(vmem, vmem),
        scratch_shapes=scratch,
        compiler_params=pltpu.CompilerParams(collective_id=0, has_side_effects=True, vmem_limit_bytes=48 << 20),
    )(design, observations, start_coefs, precond.reshape(1, -1), taps.reshape(1, -1))


def solution(mesh):
    placed = (P("arc", "coef"), P("coef", "arc"), P("arc", "coef"), P("coef"), P())
    return jax.shard_map(
        body,
        mesh=mesh,
        in_specs=placed,
        out_specs=(P("arc", "coef"), P("coef", "arc")),
        check_vma=False,
    )
```

time: 1350 us -> 162 us (0.12)
  waiting for transfers between devices: 635 us -> 0 us
  blocking collectives: 453 us -> 0 us
  local copies, waits for them, and re-layouts: 199 us -> 5.77 us
  Pallas kernels: 0 us -> 156 us
  matrix products: 22.1 us -> 0 us
  between operations: 14.5 us -> 0.65 us
    reduce_scatter x5 -> x0, waiting for transfers between devices: 508 us -> none  [the longest x3 401 us: project(): lax.psum_scatter(jnp.dot(gathered, design.T, precision=lax.Precision.HIGH...]
    psum x5 -> x0, blocking collectives: 370 us -> none  [the longest x3 218 us: data_sum(): return lax.psum(spread(local, coef_start), ('arc', 'coef'))]
    gather x2 -> x0, local copies, waits for them, and re-layouts: 194 us -> none  [the longest x1 97.2 us: make_filters(): first = jnp.where(offset >= 0, filt[jnp.clip(offset, 0, length - 1)], 0.0)]
    pallas_call x0 -> x1, Pallas kernels: none -> 156 us  [body(): pl.pallas_call(kernel, out_shape=(jax.ShapeDtypeStruct(start_coefs.shape,...]
    all_gather x3 -> x0, waiting for transfers between devices: 112 us -> none  [project(): gathered = lax.all_gather(current, 'arc', axis=0, tiled=True)]
    all_gather x2 -> x0, blocking collectives: 83.1 us -> none  [body(): back_rows = lax.all_gather(back, 'coef', axis=0, tiled=True)]
    dot_general x17 -> x0, matrix products: 22.1 us -> none  [the longest x3 11.9 us: project(): jnp.dot(gathered, design.T, precision=lax.Precision.HIGHEST, preferred_el...]
    ppermute x6 -> x0, waiting for transfers between devices: 14.4 us -> none  [shifted(): lax.ppermute(value, axis, [(source, source + steps) for source in range(i...]
  transfers between devices with their start and end apart: 14 -> 0, of which waited for: 14 -> 0; matrix products, arithmetic and copies ran while one was open for 15% -> 0% of each run, Pallas kernels for 0% -> 0%
where the time goes in v1:
time: 162 us
  Pallas kernels  156 us (96%)
  local copies, waits for them, and re-layouts  5.77 us (4%)
    pallas_call x1, Pallas kernels, body(): pl.pallas_call(kernel, out_shape=(jax.ShapeDtypeStruct(start_coefs.shape,...  156 us
    unnamed x12, local copies, waits for them, and re-layouts  5.77 us

profile of v1, /device:TPU:24, one launch (start us, length us, event | category | flops | bytes accessed | tf_op | source)
XLA Modules:
  0.0 162.1 jit_solution(14682136729817455217)
XLA Ops:
  0.6 0.0 copy-start
  0.6 1.6 copy-done
  2.2 0.0 copy-start.1
  2.2 0.8 copy-done.1
  3.1 0.0 copy-start.2
  3.1 0.8 copy-done.2
  3.8 0.0 copy-start.3
  3.8 0.7 copy-done.3
  4.5 0.0 copy-start.4
  4.5 0.7 copy-done.4
  5.2 155.7 %shard_map.68 = (f32[16,1024]{1,0:T(8,128)S(1)}, f32[16,512]{1,0:T(8,128)S(1)}) custom-call(f32[512,1024]{1,0:T(8,128)S(1)} %copy-done, f32[16,512]{1,0:T(8,128)S(1)} %copy-done.2, f32[16,1024]{1,0:T(8,128)S(1)} %copy-done.1, f32[1,1024]{1,0:T(1,128)S(1)} %bitcast.2, f32[1,128]{1,0:T(1,128)S(1)} %bitcast.3), custom_call_target="tpu_custom_call" | custom-call | tf_op jit(solution)/shard_map/pallas_call | solution.py:469
  160.8 0.6 copy.9
  161.5 0.6 copy.10
Async XLA Ops:
  0.6 1.6 copy-start
  2.2 0.8 copy-start.1
  3.1 0.8 copy-start.2
  3.8 0.7 copy-start.3
  4.5 0.7 copy-start.4

commit v2 on v1

v2 whole, which is shorter than its diff:
```python
import functools
import jax
import jax.numpy as jnp
from jax import lax
from jax.experimental import pallas as pl
from jax.experimental.pallas import tpu as pltpu
from jax.sharding import PartitionSpec as P

ITERS = 2
TOTAL_OBS = 8192
HUBER_SQUARE = 2.25
EPSILON = 1e-06

F32 = jnp.float32
BF16 = jnp.bfloat16
MESH = pl.DeviceIdType.MESH


def split(value):
    high = value.astype(BF16)
    low = (value - high.astype(F32)).astype(BF16)
    return high, low


def dot3(value, weight_high, weight_low):
    rows = value.shape[0]
    high, low = split(value)
    both = jnp.dot(jnp.concatenate([high, low], axis=0), weight_high, preferred_element_type=F32)
    rest = jnp.dot(high, weight_low, preferred_element_type=F32)
    return both[:rows] + both[rows:] + rest


def lanes(value):
    total = value[:, 0:128]
    for start in range(128, value.shape[1], 128):
        total = total + value[:, start:start + 128]
    return total


def fold(values):
    group = lax.broadcasted_iota(jnp.int32, (8, 128), 1) // 16
    tile = jnp.zeros((8, 128), F32)
    for n, value in enumerate(values):
        for shift in (64, 32, 16):
            value = value + pltpu.roll(value, shift, 1)
        tile = jnp.where(group == 2 * n, value[0:8], tile)
        tile = jnp.where(group == 2 * n + 1, value[8:16], tile)
    return tile


def unfold(tile, count):
    for shift in (8, 4, 2, 1):
        tile = tile + pltpu.roll(tile, shift, 1)
    return [jnp.concatenate([tile[:, 32 * n + 15:32 * n + 16], tile[:, 32 * n + 31:32 * n + 32]], axis=0) for n in range(count)]


def pack(one, two):
    lane = lax.broadcasted_iota(jnp.int32, (8, 128), 1)
    return jnp.where(lane < 64, jnp.where(lane < 32, one[0:8], one[8:16]), jnp.where(lane < 96, two[0:8], two[8:16]))


def unpack(tile, which):
    start = 64 * which
    return jnp.concatenate([tile[:, start:start + 1], tile[:, start + 32:start + 33]], axis=0)


def filter_blocks(extended):
    return jnp.concatenate([extended[:, j * 128:(j + 2) * 128] for j in range(4)], axis=0)


def unblock(value):
    return jnp.concatenate([value[j * 16:(j + 1) * 16] for j in range(4)], axis=1)


def kernel(design_hbm, obs_hbm, start_hbm, precond_hbm, taps_hbm, coefs_ref, misfit_ref,
           design_f, obs_v, precond_v, taps_v, halo, d_high, d_low, g_high, g_low, t_high, t_low, w_high, w_low, filter_t,
           gather, partial, pair_part, landed, back_rows, grad_part, pair_land, grad_land,
           edge_src, edge_dst, sum_src, sum_dst, gp_src, gp_dst, diag_gp, diag_alpha, vector,
           load_sem, halo_sem, ag_send, ag_recv, fwd_send, fwd_recv, part_send, part_recv, rs_send, rs_recv,
           bg_send, bg_recv, bf_send, bf_recv, pair_send, pair_recv, ra_send, ra_recv,
           edge_send, edge_recv, sum_send, sum_recv, gp_send, gp_recv, diag_send, diag_recv, vec_send, vec_recv):
    a = lax.axis_index("arc")
    c = lax.axis_index("coef")
    y, ma = a // 4, a % 4
    xlo, core = ma // 2, ma % 2
    yc, mc = c // 4, c % 4
    xh, z = c // 8, c % 8
    sibling = a + 1 - 2 * core
    across = (xh * 8 + 8) % 16 + z

    loads = []
    for n, (source, target) in enumerate([(start_hbm, gather.at[0, ma, y]), (taps_hbm, taps_v), (design_hbm, design_f),
                                          (obs_hbm, obs_v), (precond_hbm, precond_v)]):
        loads.append(pltpu.make_async_copy(source, target, load_sem.at[n]))
        loads[-1].start()

    barrier = pltpu.get_barrier_semaphore()

    def greet(k, carry):
        pl.semaphore_signal(barrier, inc=1, device_id=((a + k) % 16, c), device_id_type=MESH)
        pl.semaphore_signal(barrier, inc=1, device_id=(a, (c + k) % 16), device_id_type=MESH)
        return carry

    lax.fori_loop(1, 16, greet, 0)

    def remote(src, dst, send, recv, device):
        return pltpu.make_async_remote_copy(src_ref=src, dst_ref=dst, send_sem=send, recv_sem=recv,
                                            device_id=device, device_id_type=MESH)

    def wait_bytes(ref, sem):
        pltpu.make_async_copy(ref, ref, sem).wait()

    pending = []

    def later(ref, sem, condition=None):
        pending.append((ref, sem, condition))

    def drain():
        for ref, sem, condition in pending:
            if condition is None:
                wait_bytes(ref, sem)
            else:
                pl.when(condition)(functools.partial(wait_bytes, ref, sem))

    loads[1].wait()
    row = lax.broadcasted_iota(jnp.int32, (128, 128), 0)
    col = lax.broadcasted_iota(jnp.int32, (128, 128), 1)
    lead = lax.broadcasted_iota(jnp.int32, (1, 128), 1)
    filt = taps_v[...] + jnp.where(lead == 0, 1.0, 0.0)
    rolled = jnp.broadcast_to(filt, (128, 128))
    for bit in range(7):
        rolled = jnp.where((row // (1 << bit)) % 2 == 1, pltpu.roll(rolled, 1 << bit, 1), rolled)
    first = jnp.where(col >= row, rolled, 0.0)
    second = jnp.where(col < row, rolled, 0.0)
    high, low = split(jnp.concatenate([second, first], axis=0))
    w_high[...] = high
    w_low[...] = low
    high, low = split(jnp.concatenate([second.T, first.T], axis=1))
    filter_t[...] = jnp.concatenate([high, low], axis=0)

    loads[0].wait()
    pl.semaphore_wait(barrier, 30)

    def along_y(p, m, i):
        for ky in (1, 3, 2):
            target = ((y + ky) % 4) * 4 + ma
            remote(gather.at[p, m, y], gather.at[p, m, y], ag_send.at[p], ag_recv.at[p, i * 4 + ky], (target, c)).start()

    def gather_arc(p):
        own = gather.at[p, ma, y]
        remote(own, own, ag_send.at[p], ag_recv.at[p, 4], (y * 4 + (ma + 2) % 4, c)).start()
        along_y(p, ma, 0)
        remote(own, own, fwd_send.at[p], fwd_recv.at[p, 0], (sibling, c)).start()
        later(landed.at[0:2, 0:7], ag_send.at[p])

    def forward(p):
        wait_bytes(gather.at[p, (ma + 2) % 4, y], ag_recv.at[p, 4])
        along_y(p, (ma + 2) % 4, 1)

        def block_of(s):
            return ((xlo + s // 2) % 2) * 2 + (core + s % 2) % 2

        def finish(s):
            m = block_of(s)
            wait_bytes(pair_part.at[p, m], part_recv.at[p, m])
            for h in range(2):
                at = 2 * xh + h
                partial[p, m, at] = partial[p, m, at] + pair_part[p, m, h]

                @pl.when(4 * h + m != z)
                def _():
                    remote(partial.at[p, m, at], landed.at[p, (4 * h + m + 8 - z) % 8], rs_send.at[p], rs_recv.at[p],
                           (a, xh * 8 + 4 * h + m)).start()

        def step(s, carry):
            i, j = s // 2, s % 2
            m = block_of(s)

            @pl.when(j == 0)
            def _():
                for ky in range(4):
                    block = gather.at[p, m, (y + 4 - ky) % 4]
                    if ky == 0:
                        @pl.when(i > 0)
                        def _():
                            remote(block, block, fwd_send.at[p], fwd_recv.at[p, i], (sibling, c)).start()
                    else:
                        wait_bytes(block, ag_recv.at[p, i * 4 + ky])
                        remote(block, block, fwd_send.at[p], fwd_recv.at[p, i], (sibling, c)).start()

            @pl.when(j == 1)
            def _():
                wait_bytes(gather.at[p, m], fwd_recv.at[p, i])

            product = dot3(gather[p, m].reshape(64, 1024), t_high[...], t_low[...])
            partial[p, m] = product.reshape(4, 16, 512)
            remote(partial.at[p, m, pl.ds(2 - 2 * xh, 2)], pair_part.at[p, m], part_send.at[p], part_recv.at[p, m], (a, across)).start()

            @pl.when(s >= 2)
            def _():
                finish(s - 2)
            return carry

        lax.fori_loop(0, 4, step, 0)
        finish(2)
        finish(3)
        later(gather.at[p, 0:2], fwd_send.at[p])
        later(pair_part.at[p], part_send.at[p])
        later(landed.at[p, 1:8], rs_send.at[p])

    def forward_sum(p):
        wait_bytes(landed.at[p, 1:8], rs_recv.at[p])
        total = partial[p, mc, yc]
        for k in range(1, 8):
            total = total + landed[p, k]
        return total

    def gather_coef(it):
        own = back_rows.at[it, mc, yc]
        remote(own, own, bf_send.at[it], bf_recv.at[it], (a, across)).start()
        for dz in (1, 7, 2, 6, 3, 5, 4):
            remote(own, own, bg_send.at[it], bg_recv.at[it, dz], (a, xh * 8 + (z + dz) % 8)).start()

    def gather_coef_on(it):
        for dz in (1, 7, 2, 6, 3, 5, 4):
            source = (z + 8 - dz) % 8
            block = back_rows.at[it, source % 4, 2 * xh + source // 4]
            wait_bytes(block, bg_recv.at[it, dz])
            remote(block, block, bf_send.at[it], bf_recv.at[it], (a, across)).start()
        wait_bytes(back_rows.at[it, 0:2], bf_recv.at[it])
        later(landed.at[it, 1:8], bg_send.at[it])
        later(back_rows.at[it, 0:2], bf_send.at[it])

    def spread(it, one, two):
        own = vector.at[it, mc, yc]
        own[...] = pack(one, two)

        def step(k, carry):
            remote(own, own, vec_send.at[it], vec_recv.at[it], (a, (c + k) % 16)).start()
            return carry

        lax.fori_loop(1, 16, step, 0)
        later(sum_dst.at[it, 1:16], vec_send.at[it])

    def spread_wait(it):
        wait_bytes(sum_dst.at[it, 1:16], vec_recv.at[it])

    def spread_rows(it, m, which):
        return jnp.concatenate([unpack(vector[it, m, k], which) for k in range(4)], axis=0)

    def weighted_rows(it, m):
        rows = back_rows[0, m].reshape(64, 512)
        if it == 0:
            return rows * lax.rsqrt(1.0 + rows * rows * spread_rows(0, m, 0))
        rows = rows - spread_rows(1, m, 0) * back_rows[1, m].reshape(64, 512)
        return rows * lax.rsqrt(1.0 + rows * rows * spread_rows(1, m, 1))

    def backward(it):
        def finish(i):
            xl = (xlo + i) % 2
            m = 2 * xl + core
            wait_bytes(pair_land.at[it, xl], pair_recv.at[it, xl])
            grad_part[it, m] = grad_part[it, m] + pair_land[it, xl]
            for ky in (1, 3, 2, 0):
                ty = (y + ky) % 4
                if ky == 0 and i == 0:
                    continue
                remote(grad_part.at[it, m, ty], grad_land.at[it, i * 4 + ky], ra_send.at[it], ra_recv.at[it], (ty * 4 + m, c)).start()

        def step(s, carry):
            i, j = 1 - s // 2, 1 - s % 2
            xl = (xlo + i) % 2
            m = 2 * xl + (core + j) % 2
            product = dot3(weighted_rows(it, m), g_high[...], g_low[...])
            grad_part[it, m] = product.reshape(4, 16, 1024)

            @pl.when(j == 1)
            def _():
                remote(grad_part.at[it, m], pair_land.at[it, xl], pair_send.at[it, xl], pair_recv.at[it, xl], (sibling, c)).start()

            @pl.when(s == 2)
            def _():
                finish(1)
            return carry

        lax.fori_loop(0, 4, step, 0)
        finish(0)
        for xl in range(2):
            later(pair_land.at[it, xl], pair_send.at[it, xl])
        later(grad_land.at[it, 1:8], ra_send.at[it])

    def backward_sum(it):
        wait_bytes(grad_land.at[it, 1:8], ra_recv.at[it])
        total = grad_part[it, ma, y]
        for k in range(1, 8):
            total = total + grad_land[it, k]
        return total

    def whiten(n, value):
        edge_src[n] = value[:, 384:512]

        @pl.when(a < 15)
        def _():
            remote(edge_src.at[n], edge_dst.at[n], edge_send.at[n], edge_recv.at[n], (a + 1, c)).start()

        later(edge_src.at[n], edge_send.at[n], a < 15)

        @pl.when(a == 0)
        def _():
            edge_dst[n] = jnp.zeros((16, 128), F32)

        inside = filter_blocks(jnp.concatenate([jnp.zeros((16, 128), F32), value], axis=1))
        inside = unblock(dot3(inside, w_high[...], w_low[...]))

        @pl.when(a > 0)
        def _():
            wait_bytes(edge_dst.at[n], edge_recv.at[n])

        outside = dot3(edge_dst[n], w_high[0:128, :], w_low[0:128, :])
        return jnp.concatenate([inside[:, 0:128] + outside, inside[:, 128:512]], axis=1)

    def time_sum(n, values):
        sum_src[n] = fold([lanes(value) for value in values])

        def step(k, carry):
            remote(sum_src.at[n], sum_dst.at[n, k], sum_send.at[n], sum_recv.at[n], ((a + k) % 16, c)).start()
            return carry

        lax.fori_loop(1, 16, step, 0)
        later(sum_dst.at[n, 1:16], sum_send.at[n])

    def time_sum_wait(n, count):
        wait_bytes(sum_dst.at[n, 1:16], sum_recv.at[n])
        total = sum_src[n]
        for k in range(1, 16):
            total = total + sum_dst[n, k]
        return unfold(total, count)

    def coef_sum(it, product, old):
        gp_src[it] = fold([lanes(product), lanes(old)])

        def step(k, carry):
            remote(gp_src.at[it], gp_dst.at[it, k], gp_send.at[it], gp_recv.at[it], (a, (c + k) % 16)).start()
            return carry

        lax.fori_loop(1, 16, step, 0)
        later(gp_dst.at[it, 1:16], gp_send.at[it])

    def coef_sum_wait(it):
        wait_bytes(gp_dst.at[it, 1:16], gp_recv.at[it])
        total = gp_src[it]
        for k in range(1, 16):
            total = total + gp_dst[it, k]

        @pl.when(a == c)
        def _():
            diag_gp[it] = total

            def step(k, carry):
                remote(diag_gp.at[it], diag_gp.at[it], diag_send.at[it], diag_recv.at[it], ((a + k) % 16, c)).start()
                return carry

            lax.fori_loop(1, 16, step, 0)
        later(gp_dst.at[it, 1:16], diag_send.at[it], a == c)
        return unfold(total, 2)

    def diag_gp_wait(it):
        @pl.when(a != c)
        def _():
            wait_bytes(diag_gp.at[it], diag_recv.at[it])
        return unfold(diag_gp[it], 2)

    def alpha_spread(alpha):
        @pl.when(a == c)
        def _():
            diag_alpha[...] = pack(alpha, alpha)

            def step(k, carry):
                remote(diag_alpha, diag_alpha, diag_send.at[ITERS], diag_recv.at[ITERS], (a, (c + k) % 16)).start()
                return carry

            lax.fori_loop(1, 16, step, 0)
        later(gp_dst.at[0, 1:16], diag_send.at[ITERS], a == c)

    def alpha_wait():
        @pl.when(a != c)
        def _():
            wait_bytes(diag_alpha, diag_recv.at[ITERS])
        return unpack(diag_alpha[...], 0)

    gather_arc(0)
    loads[2].wait()

    @pl.when(a < 15)
    def _():
        remote(design_f.at[384:512], halo, halo_sem.at[0], halo_sem.at[1], (a + 1, c)).start()

    later(halo, halo_sem.at[0], a < 15)

    @pl.when(a == 0)
    def _():
        halo[...] = jnp.zeros((128, 1024), F32)

    def prepare(r, carry):
        at = pl.ds(pl.multiple_of(r * 128, 128), 128)
        piece = design_f[at, :]
        high, low = split(piece)
        d_high[pl.ds(pl.multiple_of(r * 128 + 128, 128), 128), :] = high
        d_low[pl.ds(pl.multiple_of(r * 128 + 128, 128), 128), :] = low
        high, low = split(piece.T)
        t_high[:, at] = high
        t_low[:, at] = low
        return carry

    lax.fori_loop(0, 4, prepare, 0)
    forward(0)

    @pl.when(a > 0)
    def _():
        wait_bytes(halo, halo_sem.at[1])

    high, low = split(halo[...])
    d_high[0:128, :] = high
    d_low[0:128, :] = low

    def whiten_design(r, carry):
        at = pl.ds(pl.multiple_of(r * 128, 128), 256)
        both = jnp.dot(filter_t[...], d_high[at, :], preferred_element_type=F32)
        rest = jnp.dot(filter_t[0:128, :], d_low[at, :], preferred_element_type=F32)
        high, low = split(both[0:128] + both[128:256] + rest)
        g_high[pl.ds(pl.multiple_of(r * 128, 128), 128), :] = high
        g_low[pl.ds(pl.multiple_of(r * 128, 128), 128), :] = low
        return carry

    lax.fori_loop(0, 4, whiten_design, 0)
    loads[3].wait()
    loads[4].wait()
    residual = obs_v[...] - forward_sum(0)
    whitened = whiten(0, residual)
    time_sum(0, [whitened * whitened])
    back_rows[0, mc, yc] = whitened
    gather_coef(0)
    square, = time_sum_wait(0, 1)
    factor = 1.0 / (square * (HUBER_SQUARE / TOTAL_OBS) + EPSILON)
    spread(0, factor, factor)

    for it in range(ITERS):
        weights = lax.rsqrt(1.0 + whitened * whitened * factor)
        gather_coef_on(it)
        spread_wait(it)
        backward(it)
        gradient = backward_sum(it)
        conditioned = precond_v[...] * gradient
        gather[it + 1, ma, y] = conditioned
        gather_arc(it + 1)
        if it == 0:
            coef_sum(it, gradient * conditioned, gradient)
        else:
            coef_sum(it, gradient * conditioned, gradient * direction)
        forward(it + 1)
        gp_a, go_a = coef_sum_wait(it)
        if it == 0:
            first_direction = direction = conditioned
        else:
            direction = conditioned + (gp_a / gp_a_old) * direction
        image = forward_sum(it + 1)
        imaged = whiten(it + 1, image)
        gp_c, go_c = diag_gp_wait(it)
        if it == 0:
            time_sum(1, [weights * imaged * imaged, whitened * imaged, imaged * imaged])
            back_rows[1, mc, yc] = imaged
            gather_coef(1)
            curvature, cross, own = time_sum_wait(1, 3)
            alpha = gp_c / curvature
            square = jnp.maximum(square - 2.0 * alpha * cross + alpha * alpha * own, 0.0)
            factor = 1.0 / (square * (HUBER_SQUARE / TOTAL_OBS) + EPSILON)
            spread(1, alpha, factor)
            whitened = whitened - alpha * imaged
            gp_a_old, gp_c_old, image_old, imaged_old = gp_a, gp_c, image, imaged
        else:
            beta = gp_c / gp_c_old
            image = image + beta * image_old
            imaged = imaged + beta * imaged_old
            time_sum(2, [weights * imaged * imaged])
            curvature, = time_sum_wait(2, 1)
            alpha = (gp_c + beta * go_c) / curvature
            alpha_spread(alpha)
        residual = residual - alpha * image
    misfit_ref[...] = residual
    coefs = gather[0, ma, y] + unpack(vector[1, ma, y], 0) * first_direction
    coefs_ref[...] = coefs + alpha_wait() * direction
    drain()


def body(design, observations, start_coefs, precond, taps):
    vmem = pl.BlockSpec(memory_space=pltpu.VMEM)
    dma = pltpu.SemaphoreType.DMA
    scratch = [
        pltpu.VMEM((512, 1024), F32), pltpu.VMEM((16, 512), F32), pltpu.VMEM((1, 1024), F32), pltpu.VMEM((1, 128), F32),
        pltpu.VMEM((128, 1024), F32),
        pltpu.VMEM((640, 1024), BF16), pltpu.VMEM((640, 1024), BF16),
        pltpu.VMEM((512, 1024), BF16), pltpu.VMEM((512, 1024), BF16),
        pltpu.VMEM((1024, 512), BF16), pltpu.VMEM((1024, 512), BF16),
        pltpu.VMEM((256, 128), BF16), pltpu.VMEM((256, 128), BF16), pltpu.VMEM((256, 256), BF16),
        pltpu.VMEM((3, 4, 4, 16, 1024), F32),
        pltpu.VMEM((3, 4, 4, 16, 512), F32),
        pltpu.VMEM((3, 4, 2, 16, 512), F32),
        pltpu.VMEM((3, 8, 16, 512), F32),
        pltpu.VMEM((2, 4, 4, 16, 512), F32),
        pltpu.VMEM((2, 4, 4, 16, 1024), F32),
        pltpu.VMEM((2, 2, 4, 16, 1024), F32),
        pltpu.VMEM((2, 8, 16, 1024), F32),
        pltpu.VMEM((3, 16, 128), F32), pltpu.VMEM((3, 16, 128), F32),
        pltpu.VMEM((3, 8, 128), F32), pltpu.VMEM((3, 16, 8, 128), F32),
        pltpu.VMEM((2, 8, 128), F32), pltpu.VMEM((2, 16, 8, 128), F32),
        pltpu.VMEM((2, 8, 128), F32), pltpu.VMEM((8, 128), F32),
        pltpu.VMEM((2, 4, 4, 8, 128), F32),
        dma((5,)), dma((2,)),
        dma((3,)), dma((3, 8)), dma((3,)), dma((3, 2)), dma((3,)), dma((3, 4)), dma((3,)), dma((3,)),
        dma((2,)), dma((2, 8)), dma((2,)), dma((2,)), dma((2, 2)), dma((2, 2)), dma((2,)), dma((2,)),
        dma((3,)), dma((3,)), dma((3,)), dma((3,)), dma((2,)), dma((2,)), dma((3,)), dma((3,)), dma((2,)), dma((2,)),
    ]
    return pl.pallas_call(
        kernel,
        out_shape=(jax.ShapeDtypeStruct(start_coefs.shape, F32), jax.ShapeDtypeStruct(observations.shape, F32)),
        in_specs=[pl.BlockSpec(memory_space=pl.ANY)] * 5,
        out_specs=(vmem, vmem),
        scratch_shapes=scratch,
        compiler_params=pltpu.CompilerParams(collective_id=0, has_side_effects=True, vmem_limit_bytes=60 << 20),
    )(design, observations, start_coefs, precond.reshape(1, -1), taps.reshape(1, -1))


def solution(mesh):
    placed = (P("arc", "coef"), P("coef", "arc"), P("arc", "coef"), P("coef"), P())
    return jax.shard_map(
        body,
        mesh=mesh,
        in_specs=placed,
        out_specs=(P("arc", "coef"), P("coef", "arc")),
        check_vma=False,
    )
```

time: 162 us -> 146 us (0.901)
  Pallas kernels: 156 us -> 142 us
  local copies, waits for them, and re-layouts: 5.77 us -> 2.85 us
    pallas_call x1, Pallas kernels: 156 us -> 142 us  [body(): pl.pallas_call(kernel, out_shape=(jax.ShapeDtypeStruct(start_coefs.shape,...]
    unnamed x12 -> x2, local copies, waits for them, and re-layouts: 5.77 us -> 2.85 us
where the time goes in v2:
time: 146 us; the launch traced here: 145 us
  Pallas kernels  142 us (97%)
  local copies, waits for them, and re-layouts  2.85 us (2%)
    pallas_call x1, Pallas kernels, body(): pl.pallas_call(kernel, out_shape=(jax.ShapeDtypeStruct(start_coefs.shape,...  142 us

profile of v2, /device:TPU:24, one launch (start us, length us, event | category | flops | bytes accessed | tf_op | source)
XLA Modules:
  0.0 145.4 jit_solution(2458390230933187029)
XLA Ops:
  0.6 141.9 %shard_map.68 = (f32[16,1024]{1,0:T(8,128)}, f32[16,512]{1,0:T(8,128)}) custom-call(f32[512,1024]{1,0:T(8,128)} %design_hbm.1, f32[16,512]{1,0:T(8,128)} %obs_hbm.1, f32[16,1024]{1,0:T(8,128)} %start_hbm.1, f32[1,1024]{1,0:T(1,128)} %bitcast.2, f32[1,128]{1,0:T(1,128)} %bitcast.3), custom_call_target="tpu_custom_call" | custom-call | tf_op jit(solution)/shard_map/pallas_call | solution.py:523
  142.6 1.5 %copy.9 = f32[16,1024]{1,0:T(8,128)} copy(f32[16,1024]{1,0:T(8,128)} %get-tuple-element.4) | data formatting | bytes 131072
  144.1 1.4 copy.10

commit v3 on v2

--- a/solution.py
+++ b/solution.py
@@ -73,19 +73,21 @@
 
 
 def kernel(design_hbm, obs_hbm, start_hbm, precond_hbm, taps_hbm, coefs_ref, misfit_ref,
-           design_f, obs_v, precond_v, taps_v, halo, d_high, d_low, g_high, g_low, t_high, t_low, w_high, w_low, filter_t,
-           gather, partial, pair_part, landed, back_rows, grad_part, pair_land, grad_land,
-           edge_src, edge_dst, sum_src, sum_dst, gp_src, gp_dst, diag_gp, diag_alpha, vector,
-           load_sem, halo_sem, ag_send, ag_recv, fwd_send, fwd_recv, part_send, part_recv, rs_send, rs_recv,
-           bg_send, bg_recv, bf_send, bf_recv, pair_send, pair_recv, ra_send, ra_recv,
+           design_f, obs_v, precond_v, taps_v, halo, d_high, d_low, g_f, g_s, g_high, g_low, t_high, t_low, w_high, w_low, filter_t,
+           gather, partial, pair_part, landed, own_rows, back_rows, grad_part, grad_land,
+           edge_src, edge_dst, sum_src, sum_dst, gp_src, gp_dst, diag_gp, cur_dst, vector,
+           load_sem, halo_sem, design_sem, cur_send, cur_recv, ag_send, ag_recv, fwd_send, fwd_recv, part_send, part_recv, rs_send, rs_recv,
+           bg_send, bg_recv, bf_send, bf_recv, ra_send, ra_recv,
            edge_send, edge_recv, sum_send, sum_recv, gp_send, gp_recv, diag_send, diag_recv, vec_send, vec_recv):
     a = lax.axis_index("arc")
     c = lax.axis_index("coef")
     y, ma = a // 4, a % 4
     xlo, core = ma // 2, ma % 2
+    xh, z = c // 8, c % 8
     yc, mc = c // 4, c % 4
-    xh, z = c // 8, c % 8
+    xlc, side = mc // 2, mc % 2
     sibling = a + 1 - 2 * core
+    home = core == side
     across = (xh * 8 + 8) % 16 + z
 
     loads = []
@@ -103,6 +105,20 @@
 
     lax.fori_loop(1, 16, greet, 0)
 
+    def greet_z(k, carry):
+        pl.semaphore_signal(barrier, inc=1, device_id=(sibling, xh * 8 + (z + k) % 8), device_id_type=MESH)
+        return carry
+
+    lax.fori_loop(1, 8, greet_z, 0)
+
+    def greet_rows(k, carry):
+        @pl.when(jnp.logical_or(k != a, a != c))
+        def _():
+            pl.semaphore_signal(barrier, inc=1, device_id=(k, a), device_id_type=MESH)
+        return carry
+
+    lax.fori_loop(0, 16, greet_rows, 0)
+
     def remote(src, dst, send, recv, device):
         return pltpu.make_async_remote_copy(src_ref=src, dst_ref=dst, send_sem=send, recv_sem=recv,
                                             device_id=device, device_id_type=MESH)
@@ -114,6 +130,14 @@
 
     def later(ref, sem, condition=None):
         pending.append((ref, sem, condition))
+
+    def later_home(inside, outside, sem):
+        later(inside, sem, home)
+        later(outside, sem, jnp.logical_not(home))
+
+    def wait_home(inside, outside, sem):
+        pl.when(home)(functools.partial(wait_bytes, inside, sem))
+        pl.when(jnp.logical_not(home))(functools.partial(wait_bytes, outside, sem))
 
     def drain():
         for ref, sem, condition in pending:
@@ -139,7 +163,13 @@
     filter_t[...] = jnp.concatenate([high, low], axis=0)
 
     loads[0].wait()
-    pl.semaphore_wait(barrier, 30)
+    @pl.when(a == c)
+    def _():
+        pl.semaphore_wait(barrier, 52)
+
+    @pl.when(a != c)
+    def _():
+        pl.semaphore_wait(barrier, 53)
 
     def along_y(p, m, i):
         for ky in (1, 3, 2):
@@ -215,83 +245,82 @@
             total = total + landed[p, k]
         return total
 
-    def gather_coef(it):
-        own = back_rows.at[it, mc, yc]
-        remote(own, own, bf_send.at[it], bf_recv.at[it], (a, across)).start()
-        for dz in (1, 7, 2, 6, 3, 5, 4):
-            remote(own, own, bg_send.at[it], bg_recv.at[it, dz], (a, xh * 8 + (z + dz) % 8)).start()
+    def gather_coef(it, value):
+        own_rows[it] = value
+        own, there = own_rows.at[it], back_rows.at[it, xlc, core, yc]
+
+        @pl.when(home)
+        def _():
+            there[...] = value
+
+        for dz in (4, 3, 5, 2, 6, 1, 7):
+            remote(own, there, bg_send.at[it], bg_recv.at[it, dz, core], (a - core + side, xh * 8 + (z + dz) % 8)).start()
+
+        @pl.when(jnp.logical_not(home))
+        def _():
+            remote(own, there, bg_send.at[it], bg_recv.at[it, 0, core], (sibling, c)).start()
+
+        later_home(landed.at[it, 1:8], landed.at[it], bg_send.at[it])
 
     def gather_coef_on(it):
-        for dz in (1, 7, 2, 6, 3, 5, 4):
-            source = (z + 8 - dz) % 8
-            block = back_rows.at[it, source % 4, 2 * xh + source // 4]
-            wait_bytes(block, bg_recv.at[it, dz])
-            remote(block, block, bf_send.at[it], bf_recv.at[it], (a, across)).start()
-        wait_bytes(back_rows.at[it, 0:2], bf_recv.at[it])
-        later(landed.at[it, 1:8], bg_send.at[it])
-        later(back_rows.at[it, 0:2], bf_send.at[it])
+        odd = (core + side) % 2
+        for n in (0, 2, 1, 3):
+            for t in (0, 1):
+                dz = 2 * n + odd
+                source = (z + 8 - dz) % 8
+                block = back_rows.at[it, (source % 4) // 2, (core + t) % 2, 2 * xh + source // 4]
+                arrived = functools.partial(wait_bytes, block, bg_recv.at[it, dz, (core + t) % 2])
+                if n == 0 and t == 0:
+                    pl.when(odd == 1)(arrived)
+                else:
+                    arrived()
+                remote(block, block, bf_send.at[it], bf_recv.at[it], (a, across)).start()
+        wait_bytes(back_rows.at[it, 0], bf_recv.at[it])
+        later(back_rows.at[it, 0], bf_send.at[it])
 
     def spread(it, one, two):
-        own = vector.at[it, mc, yc]
-        own[...] = pack(one, two)
-
-        def step(k, carry):
-            remote(own, own, vec_send.at[it], vec_recv.at[it], (a, (c + k) % 16)).start()
-            return carry
-
-        lax.fori_loop(1, 16, step, 0)
-        later(sum_dst.at[it, 1:16], vec_send.at[it])
+        @pl.when(home)
+        def _():
+            own = vector.at[it, xlc, yc]
+            own[...] = pack(one, two)
+
+            def step(k, carry):
+                remote(own, own, vec_send.at[it], vec_recv.at[it], (a, (c + k) % 16)).start()
+                return carry
+
+            lax.fori_loop(1, 16, step, 0)
+        later(sum_dst.at[it, 1:16], vec_send.at[it], home)
 
     def spread_wait(it):
-        wait_bytes(sum_dst.at[it, 1:16], vec_recv.at[it])
-
-    def spread_rows(it, m, which):
-        return jnp.concatenate([unpack(vector[it, m, k], which) for k in range(4)], axis=0)
-
-    def weighted_rows(it, m):
-        rows = back_rows[0, m].reshape(64, 512)
+        wait_home(sum_dst.at[it, 1:8], sum_dst.at[it, 0:8], vec_recv.at[it])
+
+    def spread_rows(it, xl, which):
+        return jnp.concatenate([unpack(vector[it, xl, k], which) for k in range(4)], axis=0)
+
+    def weighted_rows(it, xl, half):
+        rows = back_rows[0, xl, half].reshape(64, 512)
         if it == 0:
-            return rows * lax.rsqrt(1.0 + rows * rows * spread_rows(0, m, 0))
-        rows = rows - spread_rows(1, m, 0) * back_rows[1, m].reshape(64, 512)
-        return rows * lax.rsqrt(1.0 + rows * rows * spread_rows(1, m, 1))
+            return rows * lax.rsqrt(1.0 + rows * rows * spread_rows(0, xl, 0))
+        rows = rows - spread_rows(1, xl, 0) * back_rows[1, xl, half].reshape(64, 512)
+        return rows * lax.rsqrt(1.0 + rows * rows * spread_rows(1, xl, 1))
 
     def backward(it):
-        def finish(i):
+        for i in (1, 0):
             xl = (xlo + i) % 2
-            m = 2 * xl + core
-            wait_bytes(pair_land.at[it, xl], pair_recv.at[it, xl])
-            grad_part[it, m] = grad_part[it, m] + pair_land[it, xl]
-            for ky in (1, 3, 2, 0):
-                ty = (y + ky) % 4
+            product = dot3(weighted_rows(it, xl, 0), g_high[0], g_low[0])
+            product = product + dot3(weighted_rows(it, xl, 1), g_high[1], g_low[1])
+            grad_part[it, xl] = product.reshape(4, 16, 1024)
+            for ky in (2, 1, 3, 0):
                 if ky == 0 and i == 0:
                     continue
-                remote(grad_part.at[it, m, ty], grad_land.at[it, i * 4 + ky], ra_send.at[it], ra_recv.at[it], (ty * 4 + m, c)).start()
-
-        def step(s, carry):
-            i, j = 1 - s // 2, 1 - s % 2
-            xl = (xlo + i) % 2
-            m = 2 * xl + (core + j) % 2
-            product = dot3(weighted_rows(it, m), g_high[...], g_low[...])
-            grad_part[it, m] = product.reshape(4, 16, 1024)
-
-            @pl.when(j == 1)
-            def _():
-                remote(grad_part.at[it, m], pair_land.at[it, xl], pair_send.at[it, xl], pair_recv.at[it, xl], (sibling, c)).start()
-
-            @pl.when(s == 2)
-            def _():
-                finish(1)
-            return carry
-
-        lax.fori_loop(0, 4, step, 0)
-        finish(0)
-        for xl in range(2):
-            later(pair_land.at[it, xl], pair_send.at[it, xl])
+                ty = (y + ky) % 4
+                remote(grad_part.at[it, xl, ty], grad_land.at[it, i * 4 + ky], ra_send.at[it], ra_recv.at[it],
+                       (ty * 4 + 2 * xl + core, c)).start()
         later(grad_land.at[it, 1:8], ra_send.at[it])
 
     def backward_sum(it):
         wait_bytes(grad_land.at[it, 1:8], ra_recv.at[it])
-        total = grad_part[it, ma, y]
+        total = grad_part[it, xlo, y]
         for k in range(1, 8):
             total = total + grad_land[it, k]
         return total
@@ -370,23 +399,28 @@
             wait_bytes(diag_gp.at[it], diag_recv.at[it])
         return unfold(diag_gp[it], 2)
 
-    def alpha_spread(alpha):
+    def time_sum_rows():
         @pl.when(a == c)
         def _():
-            diag_alpha[...] = pack(alpha, alpha)
-
-            def step(k, carry):
-                remote(diag_alpha, diag_alpha, diag_send.at[ITERS], diag_recv.at[ITERS], (a, (c + k) % 16)).start()
-                return carry
-
-            lax.fori_loop(1, 16, step, 0)
-        later(gp_dst.at[0, 1:16], diag_send.at[ITERS], a == c)
-
-    def alpha_wait():
-        @pl.when(a != c)
-        def _():
-            wait_bytes(diag_alpha, diag_recv.at[ITERS])
-        return unpack(diag_alpha[...], 0)
+            cur_dst[a] = sum_src[ITERS]
+
+        def step(k, carry):
+            @pl.when(jnp.logical_or(c != a, k != c))
+            def _():
+                remote(sum_src.at[ITERS], cur_dst.at[a], cur_send, cur_recv, (c, k)).start()
+            return carry
+
+        lax.fori_loop(0, 16, step, 0)
+        later(cur_dst.at[0:15], cur_send, a == c)
+        later(cur_dst, cur_send, a != c)
+
+    def time_sum_rows_wait():
+        pl.when(a == c)(functools.partial(wait_bytes, cur_dst.at[0:15], cur_recv))
+        pl.when(a != c)(functools.partial(wait_bytes, cur_dst, cur_recv))
+        total = cur_dst[0]
+        for k in range(1, 16):
+            total = total + cur_dst[k]
+        return unfold(total, 1)
 
     gather_arc(0)
     loads[2].wait()
@@ -427,19 +461,33 @@
         at = pl.ds(pl.multiple_of(r * 128, 128), 256)
         both = jnp.dot(filter_t[...], d_high[at, :], preferred_element_type=F32)
         rest = jnp.dot(filter_t[0:128, :], d_low[at, :], preferred_element_type=F32)
-        high, low = split(both[0:128] + both[128:256] + rest)
-        g_high[pl.ds(pl.multiple_of(r * 128, 128), 128), :] = high
-        g_low[pl.ds(pl.multiple_of(r * 128, 128), 128), :] = low
+        value = both[0:128] + both[128:256] + rest
+        at = pl.ds(pl.multiple_of(r * 128, 128), 128)
+        g_f[at, :] = value
+        high, low = split(value)
+        g_high[core, at, :] = high
+        g_low[core, at, :] = low
         return carry
 
     lax.fori_loop(0, 4, whiten_design, 0)
+    remote(g_f, g_s, design_sem.at[0], design_sem.at[1], (sibling, c)).start()
+    later(g_f, design_sem.at[0])
+    wait_bytes(g_s, design_sem.at[1])
+
+    def split_sibling(r, carry):
+        at = pl.ds(pl.multiple_of(r * 128, 128), 128)
+        high, low = split(g_s[at, :])
+        g_high[1 - core, at, :] = high
+        g_low[1 - core, at, :] = low
+        return carry
+
+    lax.fori_loop(0, 4, split_sibling, 0)
     loads[3].wait()
     loads[4].wait()
     residual = obs_v[...] - forward_sum(0)
     whitened = whiten(0, residual)
     time_sum(0, [whitened * whitened])
-    back_rows[0, mc, yc] = whitened
-    gather_coef(0)
+    gather_coef(0, whitened)
     square, = time_sum_wait(0, 1)
     factor = 1.0 / (square * (HUBER_SQUARE / TOTAL_OBS) + EPSILON)
     spread(0, factor, factor)
@@ -462,14 +510,15 @@
         if it == 0:
             first_direction = direction = conditioned
         else:
-            direction = conditioned + (gp_a / gp_a_old) * direction
+            beta = gp_a / gp_a_old
+            direction = conditioned + beta * direction
+            grad_dir = gp_a + beta * go_a
         image = forward_sum(it + 1)
         imaged = whiten(it + 1, image)
         gp_c, go_c = diag_gp_wait(it)
         if it == 0:
             time_sum(1, [weights * imaged * imaged, whitened * imaged, imaged * imaged])
-            back_rows[1, mc, yc] = imaged
-            gather_coef(1)
+            gather_coef(1, imaged)
             curvature, cross, own = time_sum_wait(1, 3)
             alpha = gp_c / curvature
             square = jnp.maximum(square - 2.0 * alpha * cross + alpha * alpha * own, 0.0)
@@ -482,13 +531,14 @@
             image = image + beta * image_old
             imaged = imaged + beta * imaged_old
             time_sum(2, [weights * imaged * imaged])
+            time_sum_rows()
             curvature, = time_sum_wait(2, 1)
             alpha = (gp_c + beta * go_c) / curvature
-            alpha_spread(alpha)
         residual = residual - alpha * image
     misfit_ref[...] = residual
-    coefs = gather[0, ma, y] + unpack(vector[1, ma, y], 0) * first_direction
-    coefs_ref[...] = coefs + alpha_wait() * direction
+    coefs = gather[0, ma, y] + unpack(vector[1, xlo, y], 0) * first_direction
+    curvature, = time_sum_rows_wait()
+    coefs_ref[...] = coefs + (grad_dir / curvature) * direction
     drain()
 
 
@@ -496,34 +546,36 @@
     vmem = pl.BlockSpec(memory_space=pltpu.VMEM)
     dma = pltpu.SemaphoreType.DMA
     scratch = [
-        pltpu.VMEM((512, 1024), F32), pltpu.VMEM((16, 512), F32), pltpu.VMEM((1, 1024), F32), pltpu.VMEM((1, 128), F32),
+        pltpu.VMEM((512, 1024), F32),
+        pltpu.VMEM((16, 512), F32), pltpu.VMEM((1, 1024), F32), pltpu.VMEM((1, 128), F32),
         pltpu.VMEM((128, 1024), F32),
         pltpu.VMEM((640, 1024), BF16), pltpu.VMEM((640, 1024), BF16),
-        pltpu.VMEM((512, 1024), BF16), pltpu.VMEM((512, 1024), BF16),
+        pltpu.VMEM((512, 1024), F32), pltpu.VMEM((512, 1024), F32),
+        pltpu.VMEM((2, 512, 1024), BF16), pltpu.VMEM((2, 512, 1024), BF16),
         pltpu.VMEM((1024, 512), BF16), pltpu.VMEM((1024, 512), BF16),
         pltpu.VMEM((256, 128), BF16), pltpu.VMEM((256, 128), BF16), pltpu.VMEM((256, 256), BF16),
         pltpu.VMEM((3, 4, 4, 16, 1024), F32),
         pltpu.VMEM((3, 4, 4, 16, 512), F32),
         pltpu.VMEM((3, 4, 2, 16, 512), F32),
         pltpu.VMEM((3, 8, 16, 512), F32),
-        pltpu.VMEM((2, 4, 4, 16, 512), F32),
-        pltpu.VMEM((2, 4, 4, 16, 1024), F32),
+        pltpu.VMEM((2, 16, 512), F32),
+        pltpu.VMEM((2, 2, 2, 4, 16, 512), F32),
         pltpu.VMEM((2, 2, 4, 16, 1024), F32),
         pltpu.VMEM((2, 8, 16, 1024), F32),
         pltpu.VMEM((3, 16, 128), F32), pltpu.VMEM((3, 16, 128), F32),
         pltpu.VMEM((3, 8, 128), F32), pltpu.VMEM((3, 16, 8, 128), F32),
         pltpu.VMEM((2, 8, 128), F32), pltpu.VMEM((2, 16, 8, 128), F32),
-        pltpu.VMEM((2, 8, 128), F32), pltpu.VMEM((8, 128), F32),
-        pltpu.VMEM((2, 4, 4, 8, 128), F32),
-        dma((5,)), dma((2,)),
+        pltpu.VMEM((2, 8, 128), F32), pltpu.VMEM((16, 8, 128), F32),
+        pltpu.VMEM((2, 2, 4, 8, 128), F32),
+        dma((5,)), dma((2,)), dma((2,)), dma, dma,
         dma((3,)), dma((3, 8)), dma((3,)), dma((3, 2)), dma((3,)), dma((3, 4)), dma((3,)), dma((3,)),
-        dma((2,)), dma((2, 8)), dma((2,)), dma((2,)), dma((2, 2)), dma((2, 2)), dma((2,)), dma((2,)),
-        dma((3,)), dma((3,)), dma((3,)), dma((3,)), dma((2,)), dma((2,)), dma((3,)), dma((3,)), dma((2,)), dma((2,)),
+        dma((2,)), dma((2, 8, 2)), dma((2,)), dma((2,)), dma((2,)), dma((2,)),
+        dma((3,)), dma((3,)), dma((3,)), dma((3,)), dma((2,)), dma((2,)), dma((2,)), dma((2,)), dma((2,)), dma((2,)),
     ]
     return pl.pallas_call(
         kernel,
         out_shape=(jax.ShapeDtypeStruct(start_coefs.shape, F32), jax.ShapeDtypeStruct(observations.shape, F32)),
-        in_specs=[pl.BlockSpec(memory_space=pl.ANY)] * 5,
+        in_specs=[pl.BlockSpec(memory_space=pltpu.HBM)] * 5,
         out_specs=(vmem, vmem),
         scratch_shapes=scratch,
         compiler_params=pltpu.CompilerParams(collective_id=0, has_side_effects=True, vmem_limit_bytes=60 << 20),

time: 146 us -> 141 us (0.966)
  Pallas kernels: 142 us -> 138 us
    pallas_call x1, Pallas kernels: 142 us -> 138 us  [body(): pl.pallas_call(kernel, out_shape=(jax.ShapeDtypeStruct(start_coefs.shape,...]
where the time goes in v3:
time: 141 us
  Pallas kernels  138 us (98%)
  local copies, waits for them, and re-layouts  2.85 us (2%)
    pallas_call x1, Pallas kernels, body(): pl.pallas_call(kernel, out_shape=(jax.ShapeDtypeStruct(start_coefs.shape,...  138 us
    unnamed x2, local copies, waits for them, and re-layouts  2.85 us

profile of v3, /device:TPU:24, one launch (start us, length us, event | category | flops | bytes accessed | tf_op | source)
XLA Modules:
  0.0 141.0 jit_solution(2861788439827296221)
XLA Ops:
  0.6 137.5 %shard_map.68 = (f32[16,1024]{1,0:T(8,128)}, f32[16,512]{1,0:T(8,128)}) custom-call(f32[512,1024]{1,0:T(8,128)} %design_hbm.1, f32[16,512]{1,0:T(8,128)} %obs_hbm.1, f32[16,1024]{1,0:T(8,128)} %start_hbm.1, f32[1,1024]{1,0:T(1,128)} %bitcast.2, f32[1,128]{1,0:T(1,128)} %bitcast.3), custom_call_target="tpu_custom_call" | custom-call | tf_op jit(solution)/shard_map/pallas_call | solution.py:575
  138.1 1.5 %copy.9 = f32[16,1024]{1,0:T(8,128)} copy(f32[16,1024]{1,0:T(8,128)} %get-tuple-element.4) | data formatting | bytes 131072
  139.6 1.4 copy.10

commit v4 on v3

--- a/solution.py
+++ b/solution.py
@@ -245,36 +245,43 @@
             total = total + landed[p, k]
         return total
 
-    def gather_coef(it, value):
-        own_rows[it] = value
-        own, there = own_rows.at[it], back_rows.at[it, xlc, core, yc]
+    def columns(part):
+        return pl.ds(0, 128) if part else pl.ds(128, 384)
+
+    def gather_coef(it, part, value):
+        at = columns(part)
+        own, there = own_rows.at[it, :, at], back_rows.at[it, xlc, core, yc, :, at]
+        own[...] = value
 
         @pl.when(home)
         def _():
             there[...] = value
 
         for dz in (4, 3, 5, 2, 6, 1, 7):
-            remote(own, there, bg_send.at[it], bg_recv.at[it, dz, core], (a - core + side, xh * 8 + (z + dz) % 8)).start()
+            remote(own, there, bg_send.at[it], bg_recv.at[it, part, dz, core],
+                   (a - core + side, xh * 8 + (z + dz) % 8)).start()
 
         @pl.when(jnp.logical_not(home))
         def _():
-            remote(own, there, bg_send.at[it], bg_recv.at[it, 0, core], (sibling, c)).start()
-
-        later_home(landed.at[it, 1:8], landed.at[it], bg_send.at[it])
+            remote(own, there, bg_send.at[it], bg_recv.at[it, part, 0, core], (sibling, c)).start()
+
+        if part == 1:
+            later_home(landed.at[it, 1:8], landed.at[it], bg_send.at[it])
 
     def gather_coef_on(it):
         odd = (core + side) % 2
-        for n in (0, 2, 1, 3):
-            for t in (0, 1):
-                dz = 2 * n + odd
-                source = (z + 8 - dz) % 8
-                block = back_rows.at[it, (source % 4) // 2, (core + t) % 2, 2 * xh + source // 4]
-                arrived = functools.partial(wait_bytes, block, bg_recv.at[it, dz, (core + t) % 2])
-                if n == 0 and t == 0:
-                    pl.when(odd == 1)(arrived)
-                else:
-                    arrived()
-                remote(block, block, bf_send.at[it], bf_recv.at[it], (a, across)).start()
+        for part in (0, 1):
+            for n in (0, 2, 1, 3):
+                for t in (0, 1):
+                    dz = 2 * n + odd
+                    source = (z + 8 - dz) % 8
+                    block = back_rows.at[it, (source % 4) // 2, (core + t) % 2, 2 * xh + source // 4, :, columns(part)]
+                    arrived = functools.partial(wait_bytes, block, bg_recv.at[it, part, dz, (core + t) % 2])
+                    if n == 0 and t == 0:
+                        pl.when(odd == 1)(arrived)
+                    else:
+                        arrived()
+                    remote(block, block, bf_send.at[it], bf_recv.at[it], (a, across)).start()
         wait_bytes(back_rows.at[it, 0], bf_recv.at[it])
         later(back_rows.at[it, 0], bf_send.at[it])
 
@@ -325,7 +332,7 @@
             total = total + grad_land[it, k]
         return total
 
-    def whiten(n, value):
+    def whiten(n, value, ahead=None):
         edge_src[n] = value[:, 384:512]
 
         @pl.when(a < 15)
@@ -340,6 +347,8 @@
 
         inside = filter_blocks(jnp.concatenate([jnp.zeros((16, 128), F32), value], axis=1))
         inside = unblock(dot3(inside, w_high[...], w_low[...]))
+        if ahead is not None:
+            ahead(inside[:, 128:512])
 
         @pl.when(a > 0)
         def _():
@@ -424,16 +433,6 @@
 
     gather_arc(0)
     loads[2].wait()
-
-    @pl.when(a < 15)
-    def _():
-        remote(design_f.at[384:512], halo, halo_sem.at[0], halo_sem.at[1], (a + 1, c)).start()
-
-    later(halo, halo_sem.at[0], a < 15)
-
-    @pl.when(a == 0)
-    def _():
-        halo[...] = jnp.zeros((128, 1024), F32)
 
     def prepare(r, carry):
         at = pl.ds(pl.multiple_of(r * 128, 128), 128)
@@ -448,6 +447,24 @@
 
     lax.fori_loop(0, 4, prepare, 0)
     forward(0)
+
+    @pl.when(a < 15)
+    def _():
+        remote(design_f.at[384:512], halo, halo_sem.at[0], halo_sem.at[1], (a + 1, c)).start()
+
+    later(halo, halo_sem.at[0], a < 15)
+
+    @pl.when(a == 0)
+    def _():
+        halo[...] = jnp.zeros((128, 1024), F32)
+
+
+    loads[3].wait()
+    loads[4].wait()
+    residual = obs_v[...] - forward_sum(0)
+    whitened = whiten(0, residual, functools.partial(gather_coef, 0, 0))
+    time_sum(0, [whitened * whitened])
+    gather_coef(0, 1, whitened[:, 0:128])
 
     @pl.when(a > 0)
     def _():
@@ -472,22 +489,7 @@
     lax.fori_loop(0, 4, whiten_design, 0)
     remote(g_f, g_s, design_sem.at[0], design_sem.at[1], (sibling, c)).start()
     later(g_f, design_sem.at[0])
-    wait_bytes(g_s, design_sem.at[1])
-
-    def split_sibling(r, carry):
-        at = pl.ds(pl.multiple_of(r * 128, 128), 128)
-        high, low = split(g_s[at, :])
-        g_high[1 - core, at, :] = high
-        g_low[1 - core, at, :] = low
-        return carry
-
-    lax.fori_loop(0, 4, split_sibling, 0)
-    loads[3].wait()
-    loads[4].wait()
-    residual = obs_v[...] - forward_sum(0)
-    whitened = whiten(0, residual)
-    time_sum(0, [whitened * whitened])
-    gather_coef(0, whitened)
+
     square, = time_sum_wait(0, 1)
     factor = 1.0 / (square * (HUBER_SQUARE / TOTAL_OBS) + EPSILON)
     spread(0, factor, factor)
@@ -495,6 +497,17 @@
     for it in range(ITERS):
         weights = lax.rsqrt(1.0 + whitened * whitened * factor)
         gather_coef_on(it)
+        if it == 0:
+            wait_bytes(g_s, design_sem.at[1])
+
+            def split_sibling(r, carry):
+                at = pl.ds(pl.multiple_of(r * 128, 128), 128)
+                high, low = split(g_s[at, :])
+                g_high[1 - core, at, :] = high
+                g_low[1 - core, at, :] = low
+                return carry
+
+            lax.fori_loop(0, 4, split_sibling, 0)
         spread_wait(it)
         backward(it)
         gradient = backward_sum(it)
@@ -514,11 +527,11 @@
             direction = conditioned + beta * direction
             grad_dir = gp_a + beta * go_a
         image = forward_sum(it + 1)
-        imaged = whiten(it + 1, image)
+        imaged = whiten(it + 1, image, functools.partial(gather_coef, 1, 0) if it == 0 else None)
         gp_c, go_c = diag_gp_wait(it)
         if it == 0:
             time_sum(1, [weights * imaged * imaged, whitened * imaged, imaged * imaged])
-            gather_coef(1, imaged)
+            gather_coef(1, 1, imaged[:, 0:128])
             curvature, cross, own = time_sum_wait(1, 3)
             alpha = gp_c / curvature
             square = jnp.maximum(square - 2.0 * alpha * cross + alpha * alpha * own, 0.0)
@@ -569,7 +582,7 @@
         pltpu.VMEM((2, 2, 4, 8, 128), F32),
         dma((5,)), dma((2,)), dma((2,)), dma, dma,
         dma((3,)), dma((3, 8)), dma((3,)), dma((3, 2)), dma((3,)), dma((3, 4)), dma((3,)), dma((3,)),
-        dma((2,)), dma((2, 8, 2)), dma((2,)), dma((2,)), dma((2,)), dma((2,)),
+        dma((2,)), dma((2, 2, 8, 2)), dma((2,)), dma((2,)), dma((2,)), dma((2,)),
         dma((3,)), dma((3,)), dma((3,)), dma((3,)), dma((2,)), dma((2,)), dma((2,)), dma((2,)), dma((2,)), dma((2,)),
     ]
     return pl.pallas_call(

time: 141 us -> 138 us (0.979)
  Pallas kernels: 138 us -> 134 us
    pallas_call x1, Pallas kernels: 138 us -> 134 us  [body(): pl.pallas_call(kernel, out_shape=(jax.ShapeDtypeStruct(start_coefs.shape,...]
where the time goes in v4:
time: 138 us
  Pallas kernels  134 us (97%)
  local copies, waits for them, and re-layouts  2.85 us (2%)
    pallas_call x1, Pallas kernels, body(): pl.pallas_call(kernel, out_shape=(jax.ShapeDtypeStruct(start_coefs.shape,...  134 us
    unnamed x2, local copies, waits for them, and re-layouts  2.85 us

profile of v4, /device:TPU:24, one launch (start us, length us, event | category | flops | bytes accessed | tf_op | source)
XLA Modules:
  0.0 137.6 jit_solution(8027390632550308410)
XLA Ops:
  0.6 134.1 %shard_map.68 = (f32[16,1024]{1,0:T(8,128)}, f32[16,512]{1,0:T(8,128)}) custom-call(f32[512,1024]{1,0:T(8,128)} %design_hbm.1, f32[16,512]{1,0:T(8,128)} %obs_hbm.1, f32[16,1024]{1,0:T(8,128)} %start_hbm.1, f32[1,1024]{1,0:T(1,128)} %bitcast.2, f32[1,128]{1,0:T(1,128)} %bitcast.3), custom_call_target="tpu_custom_call" | custom-call | tf_op jit(solution)/shard_map/pallas_call | solution.py:588
  134.7 1.5 %copy.9 = f32[16,1024]{1,0:T(8,128)} copy(f32[16,1024]{1,0:T(8,128)} %get-tuple-element.4) | data formatting | bytes 131072
  136.2 1.4 copy.10

commit v5 on v4

--- a/solution.py
+++ b/solution.py
@@ -72,7 +72,7 @@
     return jnp.concatenate([value[j * 16:(j + 1) * 16] for j in range(4)], axis=1)
 
 
-def kernel(design_hbm, obs_hbm, start_hbm, precond_hbm, taps_hbm, coefs_ref, misfit_ref,
+def kernel(design_hbm, obs_hbm, start_hbm, precond_hbm, taps_hbm, out_ref,
            design_f, obs_v, precond_v, taps_v, halo, d_high, d_low, g_f, g_s, g_high, g_low, t_high, t_low, w_high, w_low, filter_t,
            gather, partial, pair_part, landed, own_rows, back_rows, grad_part, grad_land,
            edge_src, edge_dst, sum_src, sum_dst, gp_src, gp_dst, diag_gp, cur_dst, vector,
@@ -357,8 +357,10 @@
         outside = dot3(edge_dst[n], w_high[0:128, :], w_low[0:128, :])
         return jnp.concatenate([inside[:, 0:128] + outside, inside[:, 128:512]], axis=1)
 
-    def time_sum(n, values):
+    def time_sum(n, values, ahead=None):
         sum_src[n] = fold([lanes(value) for value in values])
+        if ahead is not None:
+            ahead()
 
         def step(k, carry):
             remote(sum_src.at[n], sum_dst.at[n, k], sum_send.at[n], sum_recv.at[n], ((a + k) % 16, c)).start()
@@ -543,15 +545,14 @@
             beta = gp_c / gp_c_old
             image = image + beta * image_old
             imaged = imaged + beta * imaged_old
-            time_sum(2, [weights * imaged * imaged])
-            time_sum_rows()
+            time_sum(2, [weights * imaged * imaged], time_sum_rows)
             curvature, = time_sum_wait(2, 1)
             alpha = (gp_c + beta * go_c) / curvature
         residual = residual - alpha * image
-    misfit_ref[...] = residual
+    out_ref[:, 1024:1536] = residual
     coefs = gather[0, ma, y] + unpack(vector[1, xlo, y], 0) * first_direction
     curvature, = time_sum_rows_wait()
-    coefs_ref[...] = coefs + (grad_dir / curvature) * direction
+    out_ref[:, 0:1024] = coefs + (grad_dir / curvature) * direction
     drain()
 
 
@@ -585,14 +586,15 @@
         dma((2,)), dma((2, 2, 8, 2)), dma((2,)), dma((2,)), dma((2,)), dma((2,)),
         dma((3,)), dma((3,)), dma((3,)), dma((3,)), dma((2,)), dma((2,)), dma((2,)), dma((2,)), dma((2,)), dma((2,)),
     ]
-    return pl.pallas_call(
+    out = pl.pallas_call(
         kernel,
-        out_shape=(jax.ShapeDtypeStruct(start_coefs.shape, F32), jax.ShapeDtypeStruct(observations.shape, F32)),
+        out_shape=jax.ShapeDtypeStruct((16, 1536), F32),
         in_specs=[pl.BlockSpec(memory_space=pltpu.HBM)] * 5,
-        out_specs=(vmem, vmem),
+        out_specs=vmem,
         scratch_shapes=scratch,
         compiler_params=pltpu.CompilerParams(collective_id=0, has_side_effects=True, vmem_limit_bytes=60 << 20),
     )(design, observations, start_coefs, precond.reshape(1, -1), taps.reshape(1, -1))
+    return out[:, 0:1024], out[:, 1024:1536]
 
 
 def solution(mesh):

time: 138 us -> 138 us (level)
    slice x0 -> x2, local copies, waits for them, and re-layouts: none -> 2.85 us  [body(): return (out[:, 0:1024], out[:, 1024:1536])]
    unnamed x2 -> x0, local copies, waits for them, and re-layouts: 2.85 us -> none
where the time goes in v5:
time: 138 us
  Pallas kernels  134 us (97%)
  local copies, waits for them, and re-layouts  2.85 us (2%)
    pallas_call x1, Pallas kernels, body(): pl.pallas_call(kernel, out_shape=jax.ShapeDtypeStruct((16, 1536), F32), i...  134 us
    slice x2, local copies, waits for them, and re-layouts, body(): return (out[:, 0:1024], out[:, 1024:1536])  2.85 us

profile of v5, /device:TPU:24, one launch (start us, length us, event | category | flops | bytes accessed | tf_op | source)
XLA Modules:
  0.0 137.8 jit_solution(1828685598123512579)
XLA Ops:
  0.6 134.3 %shard_map.68 = f32[16,1536]{1,0:T(8,128)} custom-call(f32[512,1024]{1,0:T(8,128)} %design_hbm.1, f32[16,512]{1,0:T(8,128)} %obs_hbm.1, f32[16,1024]{1,0:T(8,128)} %start_hbm.1, f32[1,1024]{1,0:T(1,128)} %bitcast.2, f32[1,128]{1,0:T(1,128)} %bitcast.3), custom_call_target="tpu_custom_call" | custom-call | tf_op jit(solution)/shard_map/pallas_call | solution.py:589
  135.0 1.4 slice.7
  136.3 1.5 %slice.6 = f32[16,1024]{1,0:T(8,128)} slice(f32[16,1536]{1,0:T(8,128)} %shard_map.68), slice={[0:16], [0:1024]} | slice | bytes 131072 | tf_op jit(solution)/shard_map/slice | solution.py:597

commit v6 on v4

--- a/solution.py
+++ b/solution.py
@@ -146,22 +146,6 @@
             else:
                 pl.when(condition)(functools.partial(wait_bytes, ref, sem))
 
-    loads[1].wait()
-    row = lax.broadcasted_iota(jnp.int32, (128, 128), 0)
-    col = lax.broadcasted_iota(jnp.int32, (128, 128), 1)
-    lead = lax.broadcasted_iota(jnp.int32, (1, 128), 1)
-    filt = taps_v[...] + jnp.where(lead == 0, 1.0, 0.0)
-    rolled = jnp.broadcast_to(filt, (128, 128))
-    for bit in range(7):
-        rolled = jnp.where((row // (1 << bit)) % 2 == 1, pltpu.roll(rolled, 1 << bit, 1), rolled)
-    first = jnp.where(col >= row, rolled, 0.0)
-    second = jnp.where(col < row, rolled, 0.0)
-    high, low = split(jnp.concatenate([second, first], axis=0))
-    w_high[...] = high
-    w_low[...] = low
-    high, low = split(jnp.concatenate([second.T, first.T], axis=1))
-    filter_t[...] = jnp.concatenate([high, low], axis=0)
-
     loads[0].wait()
     @pl.when(a == c)
     def _():
@@ -458,6 +442,22 @@
     def _():
         halo[...] = jnp.zeros((128, 1024), F32)
 
+
+    loads[1].wait()
+    row = lax.broadcasted_iota(jnp.int32, (128, 128), 0)
+    col = lax.broadcasted_iota(jnp.int32, (128, 128), 1)
+    lead = lax.broadcasted_iota(jnp.int32, (1, 128), 1)
+    filt = taps_v[...] + jnp.where(lead == 0, 1.0, 0.0)
+    rolled = jnp.broadcast_to(filt, (128, 128))
+    for bit in range(7):
+        rolled = jnp.where((row // (1 << bit)) % 2 == 1, pltpu.roll(rolled, 1 << bit, 1), rolled)
+    first = jnp.where(col >= row, rolled, 0.0)
+    second = jnp.where(col < row, rolled, 0.0)
+    high, low = split(jnp.concatenate([second, first], axis=0))
+    w_high[...] = high
+    w_low[...] = low
+    high, low = split(jnp.concatenate([second.T, first.T], axis=1))
+    filter_t[...] = jnp.concatenate([high, low], axis=0)
 
     loads[3].wait()
     loads[4].wait()
@@ -526,12 +526,14 @@
             beta = gp_a / gp_a_old
             direction = conditioned + beta * direction
             grad_dir = gp_a + beta * go_a
+        if it > 0:
+            gp_c, go_c = diag_gp_wait(it)
         image = forward_sum(it + 1)
         imaged = whiten(it + 1, image, functools.partial(gather_coef, 1, 0) if it == 0 else None)
-        gp_c, go_c = diag_gp_wait(it)
         if it == 0:
             time_sum(1, [weights * imaged * imaged, whitened * imaged, imaged * imaged])
             gather_coef(1, 1, imaged[:, 0:128])
+            gp_c, go_c = diag_gp_wait(it)
             curvature, cross, own = time_sum_wait(1, 3)
             alpha = gp_c / curvature
             square = jnp.maximum(square - 2.0 * alpha * cross + alpha * alpha * own, 0.0)

time: 138 us -> 138 us (level)
  no operation moved by 1% of the time
where the time goes in v6:
time: 138 us; the launch traced here: 137 us
  Pallas kernels  134 us (97%)
  local copies, waits for them, and re-layouts  2.85 us (2%)
    pallas_call x1, Pallas kernels, body(): pl.pallas_call(kernel, out_shape=(jax.ShapeDtypeStruct(start_coefs.shape,...  134 us
    unnamed x2, local copies, waits for them, and re-layouts  2.85 us

profile of v6, /device:TPU:24, one launch (start us, length us, event | category | flops | bytes accessed | tf_op | source)
XLA Modules:
  0.0 137.4 jit_solution(8404240272954181183)
XLA Ops:
  0.6 133.9 %shard_map.68 = (f32[16,1024]{1,0:T(8,128)}, f32[16,512]{1,0:T(8,128)}) custom-call(f32[512,1024]{1,0:T(8,128)} %design_hbm.1, f32[16,512]{1,0:T(8,128)} %obs_hbm.1, f32[16,1024]{1,0:T(8,128)} %start_hbm.1, f32[1,1024]{1,0:T(1,128)} %bitcast.2, f32[1,128]{1,0:T(1,128)} %bitcast.3), custom_call_target="tpu_custom_call" | custom-call | tf_op jit(solution)/shard_map/pallas_call | solution.py:590
  134.6 1.5 %copy.9 = f32[16,1024]{1,0:T(8,128)} copy(f32[16,1024]{1,0:T(8,128)} %get-tuple-element.4) | data formatting | bytes 131072
  136.0 1.4 copy.10

commit v7 on v6

--- a/solution.py
+++ b/solution.py
@@ -252,20 +252,23 @@
         if part == 1:
             later_home(landed.at[it, 1:8], landed.at[it], bg_send.at[it])
 
+    def pass_on(it, part, steps):
+        odd = (core + side) % 2
+        for n in steps:
+            for t in (0, 1):
+                dz = 2 * n + odd
+                source = (z + 8 - dz) % 8
+                block = back_rows.at[it, (source % 4) // 2, (core + t) % 2, 2 * xh + source // 4, :, columns(part)]
+                arrived = functools.partial(wait_bytes, block, bg_recv.at[it, part, dz, (core + t) % 2])
+                if n == 0 and t == 0:
+                    pl.when(odd == 1)(arrived)
+                else:
+                    arrived()
+                remote(block, block, bf_send.at[it], bf_recv.at[it], (a, across)).start()
+
     def gather_coef_on(it):
-        odd = (core + side) % 2
-        for part in (0, 1):
-            for n in (0, 2, 1, 3):
-                for t in (0, 1):
-                    dz = 2 * n + odd
-                    source = (z + 8 - dz) % 8
-                    block = back_rows.at[it, (source % 4) // 2, (core + t) % 2, 2 * xh + source // 4, :, columns(part)]
-                    arrived = functools.partial(wait_bytes, block, bg_recv.at[it, part, dz, (core + t) % 2])
-                    if n == 0 and t == 0:
-                        pl.when(odd == 1)(arrived)
-                    else:
-                        arrived()
-                    remote(block, block, bf_send.at[it], bf_recv.at[it], (a, across)).start()
+        pass_on(it, 0, (1, 3))
+        pass_on(it, 1, (0, 2, 1, 3))
         wait_bytes(back_rows.at[it, 0], bf_recv.at[it])
         later(back_rows.at[it, 0], bf_send.at[it])
 
@@ -490,6 +493,7 @@
     remote(g_f, g_s, design_sem.at[0], design_sem.at[1], (sibling, c)).start()
     later(g_f, design_sem.at[0])
 
+    pass_on(0, 0, (0, 2))
     square, = time_sum_wait(0, 1)
     factor = 1.0 / (square * (HUBER_SQUARE / TOTAL_OBS) + EPSILON)
     spread(0, factor, factor)
@@ -533,6 +537,7 @@
         if it == 0:
             time_sum(1, [weights * imaged * imaged, whitened * imaged, imaged * imaged])
             gather_coef(1, 1, imaged[:, 0:128])
+            pass_on(1, 0, (0, 2))
             gp_c, go_c = diag_gp_wait(it)
             curvature, cross, own = time_sum_wait(1, 3)
             alpha = gp_c / curvature

time: 138 us -> 133 us (0.964)
  Pallas kernels: 134 us -> 130 us
    pallas_call x1, Pallas kernels: 134 us -> 130 us  [body(): pl.pallas_call(kernel, out_shape=(jax.ShapeDtypeStruct(start_coefs.shape,...]
where the time goes in v7:
time: 133 us
  Pallas kernels  130 us (98%)
  local copies, waits for them, and re-layouts  2.85 us (2%)
    pallas_call x1, Pallas kernels, body(): pl.pallas_call(kernel, out_shape=(jax.ShapeDtypeStruct(start_coefs.shape,...  130 us
    unnamed x2, local copies, waits for them, and re-layouts  2.85 us

profile of v7, /device:TPU:24, one launch (start us, length us, event | category | flops | bytes accessed | tf_op | source)
XLA Modules:
  0.0 133.2 jit_solution(10437644956525026934)
XLA Ops:
  0.6 129.8 %shard_map.68 = (f32[16,1024]{1,0:T(8,128)}, f32[16,512]{1,0:T(8,128)}) custom-call(f32[512,1024]{1,0:T(8,128)} %design_hbm.1, f32[16,512]{1,0:T(8,128)} %obs_hbm.1, f32[16,1024]{1,0:T(8,128)} %start_hbm.1, f32[1,1024]{1,0:T(1,128)} %bitcast.2, f32[1,128]{1,0:T(1,128)} %bitcast.3), custom_call_target="tpu_custom_call" | custom-call | tf_op jit(solution)/shard_map/pallas_call | solution.py:595
  130.4 1.5 %copy.9 = f32[16,1024]{1,0:T(8,128)} copy(f32[16,1024]{1,0:T(8,128)} %get-tuple-element.4) | data formatting | bytes 131072
  131.9 1.4 %copy.10 = f32[16,512]{1,0:T(8,128)} copy(f32[16,512]{1,0:T(8,128)} %get-tuple-element.5) | data formatting | bytes 65536
